TPU v7x, 256 devices: a whole 4x4x8 slice. The times are simulated.
256 devices in a mesh: lat: 8 (over z), lon: 32 (over x, y, core).
Axes of the slice: x: 4, y: 4, z: 8, core: 2. Of those that a mesh axis runs over, the one named last changes fastest.
Arguments:
- thickness: float32 [16, 512, 11520], P(None, 'lat', 'lon'), may hold values from 0.5 to 1.5
- wind: float32 [2, 16, 512, 11520], P(None, None, 'lat', 'lon'), may hold values from -6 to 6
- cutoff: int32 [256], replicated, may hold values from 1 to 2880, as said below
Outputs:
- thick_out: float32 [16, 512, 11520], P(None, 'lat', 'lon')
- wind_out: float32 [2, 16, 512, 11520], P(None, None, 'lat', 'lon')
Inputs may be any that keep to these rules, and one draw needn't show every extreme that they name: `cutoff`: some row keeps exactly 2880 and some row exactly 1.
All inputs are finite; a program needn't handle non-finite values.
Results may differ from a plain program's by a relative error of at most 0.000075.
Values sent between devices are 32-bit elements; how exact they have to be, the bound alone decides.
A program may use at most 128 MiB of HBM per device.

v0:
```python
import math

import jax
import jax.numpy as jnp
import numpy as np
from jax import lax
from jax.sharding import PartitionSpec as P

advect_coef = 0.05
press_coef = 0.1
RANK = 24


def cauchy_tables(columns, count):
    total = columns * count
    inside = np.arange(columns)
    outside = np.arange(columns, total)
    far = 1.0 / (total * np.sin(np.pi * (inside[:, None] - outside[None]) / total))
    basis = np.linalg.svd(far, full_matrices=False)[0][:, :RANK]
    gap = inside[:, None] - inside[None]
    near = np.where(gap == 0, 0.0, 1.0 / (total * np.sin(np.pi * gap / total) + (gap == 0)))
    cross = np.zeros((count, RANK, count, RANK))
    for shift in range(1 - count, count):
        if shift == 0:
            continue
        piece = basis.T @ (1.0 / (total * np.sin(np.pi * (gap + shift * columns) / total))) @ basis
        for p in range(count):
            q = p - shift
            if 0 <= q < count:
                cross[p, :, q, :] = piece
    return near, basis, cross


def padded(cells, sides, width, closed):
    for axis, dim in sides:
        count = lax.axis_size(axis)
        ends = count if closed else count - 1
        head = lax.slice_in_dim(cells, 0, width, axis=dim)
        tail = lax.slice_in_dim(cells, cells.shape[dim] - width, cells.shape[dim], axis=dim)
        cells = jnp.concatenate(
            [
                lax.ppermute(tail, axis, [(i, (i + 1) % count) for i in range(ends)]),
                cells,
                lax.ppermute(head, axis, [((i + 1) % count, i) for i in range(ends)]),
            ],
            axis=dim,
        )
    return cells


def smooth(block, cuts):
    items, rows, columns = block.shape
    count = lax.axis_size("lon")
    total = columns * count
    near, basis, cross = cauchy_tables(columns, count)
    near = jnp.asarray(near, jnp.float32)
    basis = jnp.asarray(basis, jnp.float32)
    cross = jnp.asarray(cross, jnp.float32)
    high = lax.Precision.HIGH
    column = lax.axis_index("lon") * columns + lax.broadcasted_iota(jnp.int32, (rows, columns), 1)
    odd = (2 * cuts + 1)[:, None]
    angle = (odd * column % (2 * total)).astype(jnp.float32) * (math.pi / total)
    turn = jnp.stack([jnp.cos(angle), jnp.sin(angle)])
    waves = (block[None] * turn[:, None]).reshape(2 * items * rows, columns)
    short = jnp.einsum("nl,lf->nf", waves, basis, precision=high)
    group = items * rows // count
    short = short.reshape(2, count, group, RANK).transpose(1, 0, 2, 3).reshape(count, 2 * group, RANK)
    short = lax.all_to_all(short, "lon", split_axis=0, concat_axis=0, tiled=True)
    local = jnp.einsum("nl,ml->nm", waves, near, precision=high)
    moved = jnp.einsum("qnf,pgqf->png", short, cross, precision=high)
    moved = lax.all_to_all(moved, "lon", split_axis=0, concat_axis=0, tiled=True)
    moved = moved.reshape(count, 2, group, RANK).transpose(1, 0, 2, 3).reshape(2 * items * rows, RANK)
    parts = (local + jnp.einsum("nf,lf->nl", moved, basis, precision=high)).reshape(2, items, rows, columns)
    own = odd.astype(jnp.float32) / total
    return turn[1] * parts[0] - turn[0] * parts[1] + own * block


def edge_cells(lon_field, lat_field):
    lon_ext = padded(lon_field, (("lon", 2),), 1, True)
    lat_ext = padded(lat_field, (("lat", 1),), 1, False)
    return (lon_ext, lat_ext)


def body(thickness, wind, cutoff):
    levels, band_rows, columns = thickness.shape
    lat_count = lax.axis_size("lat")
    lat_index = lax.axis_index("lat")
    full_lat = band_rows * lat_count
    global_rows = lat_index * band_rows + lax.broadcasted_iota(jnp.int32, (band_rows, 1), 0)
    latitude = jnp.pi * ((global_rows.astype(jnp.float32) + 0.5) / full_lat - 0.5)
    cosine = jnp.cos(latitude)
    metric = 1.0 / jnp.maximum(cosine, 0.2)
    east_wind = wind[0]
    north_wind = wind[1]
    flux_lon = thickness * east_wind
    flux_lat = thickness * north_wind * cosine
    lon_ext, lat_ext = edge_cells(flux_lon, flux_lat)
    advected = thickness - advect_coef * metric * (
        lon_ext[:, :, 2:] - lon_ext[:, :, :-2] + (lat_ext[:, 2:] - lat_ext[:, :-2])
    )
    stacked = jnp.concatenate([advected[None], wind], 0).reshape(3 * levels, band_rows, columns)
    quarter = full_lat // 4
    full_cut = jnp.concatenate(
        [
            cutoff[:quarter],
            jnp.zeros((full_lat - 2 * quarter,), jnp.int32),
            cutoff[quarter:],
        ]
    )
    row_cuts = lax.dynamic_slice_in_dim(full_cut, lat_index * band_rows, band_rows)
    polar = (global_rows < quarter) | (global_rows >= full_lat - quarter)
    filtered = jnp.where(polar, smooth(stacked, row_cuts), stacked)
    thick_out = filtered[:levels]
    east_filt = filtered[levels : 2 * levels]
    north_filt = filtered[2 * levels :]
    lon_h, lat_h = edge_cells(thick_out, thick_out)
    east_out = east_filt - press_coef * metric * (lon_h[:, :, 2:] - lon_h[:, :, :-2])
    north_out = north_filt - press_coef * (lat_h[:, 2:] - lat_h[:, :-2])
    return (thick_out, jnp.stack([east_out, north_out], 0))


def solution(mesh):
    in_specs = (P(None, "lat", "lon"), P(None, None, "lat", "lon"), P())
    out_specs = (P(None, "lat", "lon"), P(None, None, "lat", "lon"))
    return jax.shard_map(body, mesh=mesh, in_specs=in_specs, out_specs=out_specs, check_vma=False)
```

profile of v0, /device:TPU:96, one launch (start us, length us, event | category | flops | bytes accessed | tf_op | source)
XLA Modules:
  0.0 132.2 jit_solution(13738385296297790513)
XLA Ops:
  0.7 2.7 %bitcast_multiply_fusion.1 = (f32[16,64,360]{2,1,0:T(8,128)S(1)}, f32[16,64,360]{2,1,0:T(8,128)S(1)}) fusion(f32[16,64,360]{2,1,0:T(8,128)} %param.6, f32[2,16,64,360]{3,2,1,0:T(8,128)} %param.7, f32[64]{0:T(128)S(1)} %multiply_cosine_fusion), kind=kLoop, calls=%fused_computation.32 | loop fusion | flops 1105920 | bytes 7373056 | tf_op jit(solution)/shard_map/mul | solution.py:95
  3.4 0.0 copy-start.6
  3.4 1.1 fusion.39
  4.6 4.6 %collective-permute-start = (f32[16,64,1]{2,1,0:T(8,128)}, f32[16,64,1]{2,1,0:T(8,128)}, u32[]{:S(2)}, u32[]{:S(2)}) collective-permute-start(f32[16,64,1]{2,1,0:T(8,128)} %get-tuple-element.14), channel_id=1, source_target_pairs={{1,0},{2,1},{3,2},{4,3},{5,4},{6,5},{7,6},{8,7},{9,8},{10,9},{11,1... | collective-permute-start | bytes 12296 | tf_op jit(solution)/shard_map/ppermute | solution.py:44
  9.2 0.0 collective-permute-start.1
  9.2 0.6 fusion.40
  9.9 2.0 %collective-permute-start.2 = (f32[16,1,360]{2,1,0:T(1,128)}, f32[16,1,360]{2,1,0:T(1,128)}, u32[]{:S(2)}, u32[]{:S(2)}) collective-permute-start(f32[16,1,360]{2,1,0:T(1,128)} %get-tuple-element.16), channel_id=1, source_target_pairs={{32,0},{64,32},{96,64},{128,96},{160,128},{192,160},{224,192},{33,... | collective-permute-start | bytes 69128 | tf_op jit(solution)/shard_map/ppermute | solution.py:44
  11.9 5.0 %collective-permute-start.3 = (f32[16,1,360]{2,1,0:T(1,128)}, f32[16,1,360]{2,1,0:T(1,128)}, u32[]{:S(2)}, u32[]{:S(2)}) collective-permute-start(f32[16,1,360]{2,1,0:T(1,128)} %get-tuple-element.17), channel_id=1, source_target_pairs={{0,32},{32,64},{64,96},{96,128},{128,160},{160,192},{192,224},{1,3... | collective-permute-start | bytes 69128 | tf_op jit(solution)/shard_map/ppermute | solution.py:42
  16.9 0.1 broadcast_multiply_fusion.2
  17.0 0.0 copy-done.6
  17.0 0.1 convert_multiply_fusion
  17.1 0.5 fusion.29
  17.6 0.5 fusion.33
  18.1 0.0 collective-permute-done
  18.1 3.3 %collective-permute-done.1 = f32[16,64,1]{2,1,0:T(8,128)} collective-permute-done((f32[16,64,1]{2,1,0:T(8,128)}, f32[16,64,1]{2,1,0:T(8,128)}, u32[]{:S(2)}, u32[]{:S(2)}) %collective-permute-start.1) | collective-permute-done | bytes 4128 | tf_op jit(solution)/shard_map/ppermute | solution.py:42
  21.4 0.0 collective-permute-done.2
  21.4 0.0 collective-permute-done.3
  21.5 0.0 copy-start.1
  21.5 2.9 %fusion.15 = f32[1,16,64,360]{3,2,1,0:T(8,128)S(1)} fusion(f32[16,64,360]{2,1,0:T(8,128)} %param.6, f32[16,64,360]{2,1,0:T(8,128)S(1)} %get-tuple-element.13, f32[16,1,360]{2,1,0:T(1,128)} %collective-permute-done.3, f32[16,1,360]{2,1,0:T(1,128)} %collective-permute-done.2, f32[16,64,360]{2,1,0:T(8,128)S(1)} %get-tuple-element.12, ...), kind=kLoop, calls=%fused_computation.25 | loop fusion | flops 3317760 | bytes 5952768 | tf_op jit(solution)/shard_map/broadcast_in_dim | solution.py:101
  24.3 0.0 copy-done.1
  24.4 0.3 pad_maximum_fusion
  24.7 0.0 copy-start
  24.7 0.0 copy-start.5
  24.7 1.2 mul.218
  25.9 1.0 copy-done
  26.9 0.0 copy-done.5
  26.9 5.8 %fusion.18 = f32[32,2,96,24]{2,3,0,1:T(8,128)S(1)} fusion(f32[360,24,1,1]{0,1,3,2:T(8,128)S(1)} %copy-done.5, f32[2,32,96,360]{3,2,1,0:T(8,128)S(1)} %bitcast.52, f32[32,96,360]{2,1,0:T(8,128)S(1)} %bitcast.49), kind=kOutput, calls=%fused_computation.33 | convolution fusion | flops 320716800 | bytes 13895424 | tf_op jit(solution)/shard_map/nl,lf->nf/dot_general | solution.py:65
  32.7 0.6 copy.15
  33.3 1.3 %reshape.190 = f32[32,192,24]{1,2,0:T(8,128)} reshape(f32[32,2,96,24]{2,1,3,0:T(2,128)S(1)} %copy.15) | data formatting | bytes 1179648 | tf_op jit(solution)/shard_map/reshape | solution.py:67
  34.6 4.1 %all-to-all-start = ((f32[32,192,24]{1,2,0:T(8,128)}), f32[32,192,24]{1,2,0:T(8,128)S(1)}, u32[]{:S(2)}, u32[]{:S(2)}) async-start(f32[32,192,24]{1,2,0:T(8,128)} %reshape.190), calls=%async_computation | async-start | bytes 1572864 | tf_op jit(solution)/shard_map/all_to_all | solution.py:68
  38.7 7.4 %broadcast_multiply_fusion = f32[2,48,64,360]{3,2,1,0:T(8,128)} fusion(f32[2,64,360]{2,1,0:T(8,128)S(1)} %pad_maximum_fusion.10, f32[48,64,360]{2,1,0:T(8,128)} %bitcast.50), kind=kLoop, calls=%fused_computation.6 | loop fusion | flops 2211840 | bytes 13455360 | tf_op jit(solution)/shard_map/mul | solution.py:64
  46.1 6.2 %all-to-all-done = f32[32,192,24]{1,2,0:T(8,128)S(1)} async-done(((f32[32,192,24]{1,2,0:T(8,128)}), f32[32,192,24]{1,2,0:T(8,128)S(1)}, u32[]{:S(2)}, u32[]{:S(2)}) %all-to-all-start) | async-done | bytes 589856 | tf_op jit(solution)/shard_map/all_to_all | solution.py:68
  52.4 11.3 %convolution_bitcast_fusion = f32[32,192,24]{1,0,2:T(8,128)S(1)} fusion(f32[32,24,32,24]{0,3,2,1:T(8,128)} %constant.72, f32[32,192,24]{1,2,0:T(8,128)S(1)} %all-to-all-done), kind=kOutput, calls=%fused_computation.34 | convolution fusion | flops 679477248 | bytes 3538944 | tf_op jit(solution)/shard_map/qnf,pgqf->png/dot_general | solution.py:70
  63.7 0.0 copy-start.3
  63.7 1.3 %copy.17 = f32[32,192,24]{1,2,0:T(8,128)} copy(f32[32,192,24]{1,0,2:T(8,128)S(1)} %convolution_bitcast_fusion) | data formatting | bytes 1179648 | tf_op jit(solution)/shard_map/qnf,pgqf->png/transpose | solution.py:70
  65.0 4.2 %all-to-all-start.1 = ((f32[32,192,24]{1,2,0:T(8,128)}), f32[32,192,24]{1,2,0:T(8,128)S(1)}, u32[]{:S(2)}, u32[]{:S(2)}) async-start(f32[32,192,24]{1,2,0:T(8,128)} %copy.17), calls=%async_computation.1 | async-start | bytes 1572864 | tf_op jit(solution)/shard_map/all_to_all | solution.py:71
  69.2 0.0 copy-done.3
  69.2 11.8 %fusion.42 = f32[6144,360]{0,1:T(8,128)} fusion(f32[6144,360]{1,0:T(8,128)} %bitcast.51, f32[360,360]{1,0:T(8,128)S(1)} %copy-done.3), kind=kOutput, calls=%fused_computation.72 | convolution fusion | flops 4777574400 | bytes 18213120 | tf_op jit(solution)/shard_map/nl,ml->nm/dot_general | solution.py:69
  81.0 2.1 %all-to-all-done.1 = f32[32,192,24]{1,2,0:T(8,128)S(1)} async-done(((f32[32,192,24]{1,2,0:T(8,128)}), f32[32,192,24]{1,2,0:T(8,128)S(1)}, u32[]{:S(2)}, u32[]{:S(2)}) %all-to-all-start.1) | async-done | bytes 589856 | tf_op jit(solution)/shard_map/all_to_all | solution.py:71
  83.1 0.5 reshape.191
  83.6 0.0 copy-start.4
  83.6 0.3 copy.27
  83.9 0.4 reshape.192
  84.3 0.1 copy-done.4
  84.4 6.3 %convolution_add_fusion = f32[6144,360]{0,1:T(8,128)S(1)} fusion(f32[6144,360]{0,1:T(8,128)} %fusion.42, f32[6144,24]{0,1:T(8,128)S(1)} %reshape.192, f32[360,24]{0,1:T(8,128)S(1)} %copy-done.4), kind=kOutput, calls=%fused_computation.2 | convolution fusion | flops 320716800 | bytes 18319104 | tf_op jit(solution)/shard_map/nf,lf->nl/dot_general | solution.py:73
  90.7 4.1 %fusion.36 = (f32[3072,360]{0,1:T(8,128)}, f32[3072,360]{0,1:T(8,128)}) fusion(f32[6144,360]{0,1:T(8,128)S(1)} %convolution_add_fusion), kind=kLoop, calls=%fused_computation.66 | loop fusion | bytes 17694720 | tf_op jit(solution)/shard_map/slice | solution.py:75
  94.8 6.0 %copy.19 = f32[3072,360]{1,0:T(8,128)} copy(f32[3072,360]{0,1:T(8,128)} %get-tuple-element.4) | data formatting | bytes 8847360 | tf_op jit(solution)/shard_map/slice | solution.py:75
  100.8 6.0 %copy.20 = f32[3072,360]{1,0:T(8,128)} copy(f32[3072,360]{0,1:T(8,128)} %get-tuple-element.5) | data formatting | bytes 8847360 | tf_op jit(solution)/shard_map/slice | solution.py:75
  106.8 6.8 %add_select_fusion = f32[48,64,360]{2,1,0:T(8,128)S(1)} fusion(f32[48,64,360]{2,1,0:T(8,128)} %bitcast.54, f32[48,64,360]{2,1,0:T(8,128)} %bitcast.53, f32[64]{0:T(128)S(1)} %get-tuple-element.2, f32[64,360]{1,0:T(8,128)S(1)} %get-tuple-element.19, f32[64,360]{1,0:T(8,128)S(1)} %get-tuple-element.18, pred[64]{0:T(512)(128)(4,1)S(1)} %compare_or_fusion, ...), kind=kLoop, calls=%fused_computation.4 | loop fusion | flops 6635520 | bytes 17879360 | tf_op jit(solution)/shard_map/jit(_where)/select_n | solution.py:112
  113.6 0.2 fusion.37
  113.8 3.0 %collective-permute-start.4 = (f32[16,64,1]{2,1,0:T(8,128)S(1)}, f32[16,64,1]{2,1,0:T(8,128)S(1)}, u32[]{:S(2)}, u32[]{:S(2)}) collective-permute-start(f32[16,64,1]{2,1,0:T(8,128)S(1)} %get-tuple-element.8), channel_id=1, source_target_pairs={{1,0},{2,1},{3,2},{4,3},{5,4},{6,5},{7,6},{8,7},{9,8},{10,9},{11,1... | collective-permute-start | bytes 12296 | tf_op jit(solution)/shard_map/ppermute | solution.py:44
  116.8 0.0 collective-permute-start.5
  116.8 2.0 %collective-permute-start.6 = (f32[16,1,360]{2,1,0:T(1,128)S(1)}, f32[16,1,360]{2,1,0:T(1,128)S(1)}, u32[]{:S(2)}, u32[]{:S(2)}) collective-permute-start(f32[16,1,360]{2,1,0:T(1,128)S(1)} %get-tuple-element.10), channel_id=1, source_target_pairs={{32,0},{64,32},{96,64},{128,96},{160,128},{192,160},{224,192},{33,... | collective-permute-start | bytes 69128 | tf_op jit(solution)/shard_map/ppermute | solution.py:44
  118.8 5.0 %collective-permute-start.7 = (f32[16,1,360]{2,1,0:T(1,128)S(1)}, f32[16,1,360]{2,1,0:T(1,128)S(1)}, u32[]{:S(2)}, u32[]{:S(2)}) collective-permute-start(f32[16,1,360]{2,1,0:T(1,128)S(1)} %get-tuple-element.11), channel_id=1, source_target_pairs={{0,32},{32,64},{64,96},{96,128},{128,160},{160,192},{192,224},{1,3... | collective-permute-start | bytes 69128 | tf_op jit(solution)/shard_map/ppermute | solution.py:42
  123.9 0.1 broadcast_multiply_fusion.1
  123.9 0.1 slice.120
  124.1 0.0 copy-start.2
  124.1 0.0 collective-permute-done.4
  124.1 4.6 %collective-permute-done.5 = f32[16,64,1]{2,1,0:T(8,128)S(1)} collective-permute-done((f32[16,64,1]{2,1,0:T(8,128)S(1)}, f32[16,64,1]{2,1,0:T(8,128)S(1)}, u32[]{:S(2)}, u32[]{:S(2)}) %collective-permute-start.5) | collective-permute-done | bytes 4128 | tf_op jit(solution)/shard_map/ppermute | solution.py:42
  128.7 0.0 collective-permute-done.6
  128.7 0.0 collective-permute-done.7
  128.7 1.4 %fusion.10 = (f32[1,16,64,360]{3,2,1,0:T(8,128)S(1)}, f32[1,16,64,360]{3,2,1,0:T(8,128)S(1)}) fusion(f32[16,64,360]{2,1,0:T(8,128)S(1)} %slice.120, f32[16,64,1]{2,1,0:T(8,128)S(1)} %collective-permute-done.5, f32[16,64,1]{2,1,0:T(8,128)S(1)} %collective-permute-done.4, f32[48,64,360]{2,1,0:T(8,128)S(1)} %add_select_fusion, ...), kind=kLoop, calls=%fused_computation.18 | loop fusion | flops 3686400 | bytes 7427328 | tf_op jit(solution)/shard_map/stack | solution.py:119
  130.2 0.0 copy-done.2
  130.2 2.0 %pad_maximum_fusion.1 = f32[2,16,64,360]{3,2,1,0:T(8,128)} fusion(f32[1,16,64,360]{3,2,1,0:T(8,128)S(1)} %get-tuple-element.7, f32[1,16,64,360]{3,2,1,0:T(8,128)S(1)} %get-tuple-element.6), kind=kLoop, calls=%fused_computation.7 | loop fusion | flops 737280 | bytes 5898240 | tf_op jit(solution)/shard_map/stack | solution.py:119
  (8 shorter events, 0.1 us)
Async XLA Ops:
  3.4 13.5 %copy-start.6 = (s32[256]{0:T(256)S(1)}, s32[256]{0:T(256)}, u32[]{:S(2)}) copy-start(s32[256]{0:T(256)} %param.8) | copy-start | bytes 3076
  4.6 13.6 %collective-permute-start = (f32[16,64,1]{2,1,0:T(8,128)}, f32[16,64,1]{2,1,0:T(8,128)}, u32[]{:S(2)}, u32[]{:S(2)}) collective-permute-start(f32[16,64,1]{2,1,0:T(8,128)} %get-tuple-element.14), channel_id=1, source_target_pairs={{1,0},{2,1},{3,2},{4,3},{5,4},{6,5},{7,6},{8,7},{9,8},{10,9},{11,1... | collective-permute-start | bytes 12296 | tf_op jit(solution)/shard_map/ppermute | solution.py:44
  9.2 12.2 %collective-permute-start.1 = (f32[16,64,1]{2,1,0:T(8,128)}, f32[16,64,1]{2,1,0:T(8,128)}, u32[]{:S(2)}, u32[]{:S(2)}) collective-permute-start(f32[16,64,1]{2,1,0:T(8,128)} %get-tuple-element.15), channel_id=1, source_target_pairs={{0,1},{1,2},{2,3},{3,4},{4,5},{5,6},{6,7},{7,8},{8,9},{9,10},{10,1... | collective-permute-start | bytes 12296 | tf_op jit(solution)/shard_map/ppermute | solution.py:42
  9.9 11.6 %collective-permute-start.2 = (f32[16,1,360]{2,1,0:T(1,128)}, f32[16,1,360]{2,1,0:T(1,128)}, u32[]{:S(2)}, u32[]{:S(2)}) collective-permute-start(f32[16,1,360]{2,1,0:T(1,128)} %get-tuple-element.16), channel_id=1, source_target_pairs={{32,0},{64,32},{96,64},{128,96},{160,128},{192,160},{224,192},{33,... | collective-permute-start | bytes 69128 | tf_op jit(solution)/shard_map/ppermute | solution.py:44
  11.9 9.6 %collective-permute-start.3 = (f32[16,1,360]{2,1,0:T(1,128)}, f32[16,1,360]{2,1,0:T(1,128)}, u32[]{:S(2)}, u32[]{:S(2)}) collective-permute-start(f32[16,1,360]{2,1,0:T(1,128)} %get-tuple-element.17), channel_id=1, source_target_pairs={{0,32},{32,64},{64,96},{96,128},{128,160},{160,192},{192,224},{1,3... | collective-permute-start | bytes 69128 | tf_op jit(solution)/shard_map/ppermute | solution.py:42
  21.5 2.9 %copy-start.1 = (f32[2,16,64,360]{3,2,1,0:T(8,128)S(1)}, f32[2,16,64,360]{3,2,1,0:T(8,128)}, u32[]{:S(2)}) copy-start(f32[2,16,64,360]{3,2,1,0:T(8,128)} %param.7) | copy-start | bytes 8847364
  24.7 2.2 %copy-start = (f32[3,16,64,360]{3,2,1,0:T(8,128)}, f32[3,16,64,360]{3,2,1,0:T(8,128)S(1)}, u32[]{:S(2)}) copy-start(f32[3,16,64,360]{3,2,1,0:T(8,128)S(1)} %pad_maximum_fusion) | copy-start | bytes 13271044
  24.7 2.2 %copy-start.5 = (f32[360,24,1,1]{0,1,3,2:T(8,128)S(1)}, f32[360,24,1,1]{0,1,3,2:T(8,128)}, u32[]{:S(2)}) copy-start(f32[360,24,1,1]{0,1,3,2:T(8,128)} %constant.71) | copy-start | bytes 103684
  34.6 17.7 %all-to-all-start = ((f32[32,192,24]{1,2,0:T(8,128)}), f32[32,192,24]{1,2,0:T(8,128)S(1)}, u32[]{:S(2)}, u32[]{:S(2)}) async-start(f32[32,192,24]{1,2,0:T(8,128)} %reshape.190), calls=%async_computation | async-start | bytes 1572864 | tf_op jit(solution)/shard_map/all_to_all | solution.py:68
  63.7 5.6 %copy-start.3 = (f32[360,360]{1,0:T(8,128)S(1)}, f32[360,360]{1,0:T(8,128)}, u32[]{:S(2)}) copy-start(f32[360,360]{1,0:T(8,128)} %constant.66.clone) | copy-start | bytes 1555204
  65.0 18.0 %all-to-all-start.1 = ((f32[32,192,24]{1,2,0:T(8,128)}), f32[32,192,24]{1,2,0:T(8,128)S(1)}, u32[]{:S(2)}, u32[]{:S(2)}) async-start(f32[32,192,24]{1,2,0:T(8,128)} %copy.17), calls=%async_computation.1 | async-start | bytes 1572864 | tf_op jit(solution)/shard_map/all_to_all | solution.py:71
  83.6 0.8 copy-start.4
  113.8 10.2 %collective-permute-start.4 = (f32[16,64,1]{2,1,0:T(8,128)S(1)}, f32[16,64,1]{2,1,0:T(8,128)S(1)}, u32[]{:S(2)}, u32[]{:S(2)}) collective-permute-start(f32[16,64,1]{2,1,0:T(8,128)S(1)} %get-tuple-element.8), channel_id=1, source_target_pairs={{1,0},{2,1},{3,2},{4,3},{5,4},{6,5},{7,6},{8,7},{9,8},{10,9},{11,1... | collective-permute-start | bytes 12296 | tf_op jit(solution)/shard_map/ppermute | solution.py:44
  116.8 11.9 %collective-permute-start.5 = (f32[16,64,1]{2,1,0:T(8,128)S(1)}, f32[16,64,1]{2,1,0:T(8,128)S(1)}, u32[]{:S(2)}, u32[]{:S(2)}) collective-permute-start(f32[16,64,1]{2,1,0:T(8,128)S(1)} %get-tuple-element.9), channel_id=1, source_target_pairs={{0,1},{1,2},{2,3},{3,4},{4,5},{5,6},{6,7},{7,8},{8,9},{9,10},{10,1... | collective-permute-start | bytes 12296 | tf_op jit(solution)/shard_map/ppermute | solution.py:42
  116.8 11.9 %collective-permute-start.6 = (f32[16,1,360]{2,1,0:T(1,128)S(1)}, f32[16,1,360]{2,1,0:T(1,128)S(1)}, u32[]{:S(2)}, u32[]{:S(2)}) collective-permute-start(f32[16,1,360]{2,1,0:T(1,128)S(1)} %get-tuple-element.10), channel_id=1, source_target_pairs={{32,0},{64,32},{96,64},{128,96},{160,128},{192,160},{224,192},{33,... | collective-permute-start | bytes 69128 | tf_op jit(solution)/shard_map/ppermute | solution.py:44
  118.8 9.9 %collective-permute-start.7 = (f32[16,1,360]{2,1,0:T(1,128)S(1)}, f32[16,1,360]{2,1,0:T(1,128)S(1)}, u32[]{:S(2)}, u32[]{:S(2)}) collective-permute-start(f32[16,1,360]{2,1,0:T(1,128)S(1)} %get-tuple-element.11), channel_id=1, source_target_pairs={{0,32},{32,64},{64,96},{96,128},{128,160},{160,192},{192,224},{1,3... | collective-permute-start | bytes 69128 | tf_op jit(solution)/shard_map/ppermute | solution.py:42
  124.1 6.1 %copy-start.2 = (f32[16,64,360]{2,1,0:T(8,128)}, f32[16,64,360]{2,1,0:T(8,128)S(1)}, u32[]{:S(2)}) copy-start(f32[16,64,360]{2,1,0:T(8,128)S(1)} %slice.120) | copy-start | bytes 4423684
where the time goes:
time: 133 us; the launch traced here: 132 us
  matrix products  35.2 us (26%)
  starting transfers between devices  30 us (23%)
  local copies, waits for them, and re-layouts  25 us (19%)
  other arithmetic  24.8 us (19%)
  waiting for transfers between devices  16.3 us (12%)
    slice x3, local copies, waits for them, and re-layouts, smooth(): return turn[1] * parts[0] - turn[0] * parts[1] + own * block  16.1 us
    dot_general x1, matrix products, smooth(): local = jnp.einsum('nl,ml->nm', waves, near, precision=high)  11.8 us
    ppermute x4, starting transfers between devices, padded(): lax.ppermute(head, axis, [((i + 1) % count, i) for i in range(ends)])  11.6 us
    dot_general x1, matrix products, smooth(): moved = jnp.einsum('qnf,pgqf->png', short, cross, precision=high)  11.3 us
    ppermute x4, starting transfers between devices, padded(): lax.ppermute(tail, axis, [(i, (i + 1) % count) for i in range(ends)])  10.1 us
    ppermute x4, waiting for transfers between devices, padded(): lax.ppermute(tail, axis, [(i, (i + 1) % count) for i in range(ends)])  7.95 us
    mul x1, other arithmetic, smooth(): waves = (block[None] * turn[:, None]).reshape(2 * items * rows, columns)  7.41 us
    select_n x1, other arithmetic, body(): filtered = jnp.where(polar, smooth(stacked, row_cuts), stacked)  6.78 us
  transfers between devices with their start and end apart: 10, of which 4 were waited for; matrix products, arithmetic and copies ran while one was open for 16% of the time, Pallas kernels for 0%

commit v1 on v0

v1 whole, which is shorter than its diff:
```python
import functools
import math

import jax
import jax.numpy as jnp
import numpy as np
from jax import lax
from jax.experimental import pallas as pl
from jax.experimental.pallas import tpu as pltpu
from jax.sharding import PartitionSpec as P

MESH = pl.DeviceIdType.MESH
F32 = jnp.float32
BF16 = jnp.bfloat16

advect_coef = 0.05
press_coef = 0.1
RANK = 24
LEVELS = 16
ROWS = 64
COLS = 360
WIDE = 384
BANDS = 8
RING = 32
TOTAL = COLS * RING
PAIRS = LEVELS // 2
CHUNKS = 3 * PAIRS
ITEMS = 2 * ROWS


def cauchy_tables():
    inside = np.arange(COLS)
    outside = np.arange(COLS, TOTAL)
    far = 1.0 / (TOTAL * np.sin(np.pi * (inside[:, None] - outside[None]) / TOTAL))
    basis = np.linalg.svd(far, full_matrices=False)[0][:, :RANK]
    gap = inside[:, None] - inside[None]
    near = np.where(gap == 0, 0.0, 1.0 / (TOTAL * np.sin(np.pi * gap / TOTAL) + (gap == 0)))
    cross = np.zeros((RING, RANK, RING, RANK))
    for shift in range(1 - RING, RING):
        if shift == 0:
            continue
        piece = basis.T @ (1.0 / (TOTAL * np.sin(np.pi * (gap + shift * COLS) / TOTAL))) @ basis
        for p in range(RING):
            if 0 <= p - shift < RING:
                cross[p, :, p - shift, :] = piece
    return near, basis, cross.reshape(RING * RANK, RING * RANK)


def two_parts(table):
    table = table.astype(np.float32)
    high = table.astype(BF16)
    low = (table - high.astype(np.float32)).astype(BF16)
    return high, low


def split(values):
    high = values.astype(BF16)
    return high, (values - high.astype(F32)).astype(BF16)


def dot(left, right, dims):
    return lax.dot_general(left, right, (dims, ((), ())), preferred_element_type=F32)


def place():
    z = lax.axis_index("lat")
    p = lax.axis_index("lon")
    return z, p


def latitude_tables(z, shape):
    row = lax.broadcasted_iota(jnp.int32, shape, 0) + z * ROWS
    latitude = math.pi * ((row.astype(F32) + 0.5) / (ROWS * BANDS) - 0.5)
    cosine = jnp.cos(latitude)
    return cosine, 1.0 / jnp.maximum(cosine, 0.2)


def worker(phase, q):
    x = q // 2
    y = 2 * (q % 2) + (x + phase % 2) % 2
    return x * 8 + y * 2 + phase // 2


def far_kernel(
    cut_ref, shrink_ref, grow_ref, th_hbm, wind_hbm, near_hbm, cross_hbm,
    ext_hbm, out_hbm,
    th, w, ext, xhi, xlo, turn, geo, wide, near, cross, u, zin, vs, vr, zhi, zlo,
    lon_out, lon_in, lat_out, lat_in,
    load_sem, u_sem, z_sem, v_sem, vr_sem, lon_sem, lonr_sem, lat_sem, latr_sem, done_sem,
):
    z, p = place()
    polar = (z < 2) | (z >= 6)
    loads = [
        pltpu.make_async_copy(wind_hbm.at[0], w.at[0], load_sem.at[0]),
        pltpu.make_async_copy(th_hbm, th, load_sem.at[1]),
        pltpu.make_async_copy(wind_hbm.at[1], w.at[1], load_sem.at[2]),
        pltpu.make_async_copy(near_hbm, near, load_sem.at[3]),
        pltpu.make_async_copy(cross_hbm, cross, load_sem.at[4]),
    ]
    for copy in loads:
        copy.start()
    barrier = pltpu.get_barrier_semaphore()

    def greet(i, carry):
        pl.semaphore_signal(barrier, inc=1, device_id=(z, (p + i) % RING), device_id_type=MESH)
        return carry

    lax.fori_loop(1, RING, greet, 0)
    for dz in (1, BANDS - 1):
        pl.semaphore_signal(barrier, inc=1, device_id=((z + dz) % BANDS, p), device_id_type=MESH)

    cosine, metric = latitude_tables(z, (ROWS, WIDE))
    for half in range(2):
        geo[0, half * ROWS : (half + 1) * ROWS] = cosine
        geo[1, half * ROWS : (half + 1) * ROWS] = advect_coef * metric
    wide[...] = jnp.zeros((ITEMS, WIDE), F32)

    @pl.when(polar)
    def _():
        band = jnp.where(z < 2, z, z - 4)
        row = lax.broadcasted_iota(jnp.int32, (ROWS, 4 * ROWS), 0) + band * ROWS
        lane = lax.broadcasted_iota(jnp.int32, (ROWS, 4 * ROWS), 1)
        cuts = jnp.broadcast_to(cut_ref[...].astype(F32), (ROWS, 4 * ROWS))
        limit = jnp.sum(jnp.where(row == lane, cuts, 0.0), axis=1, keepdims=True)
        odd = 2.0 * limit + 1.0
        column = p * COLS + lax.broadcasted_iota(jnp.int32, (ROWS, WIDE), 1)
        product = jnp.broadcast_to(odd, (ROWS, WIDE)).astype(jnp.int32) * column
        laps = jnp.floor(product.astype(F32) * (0.5 / TOTAL)).astype(jnp.int32)
        angle = (product - laps * (2 * TOTAL)).astype(F32) * (math.pi / TOTAL)
        tables = (jnp.cos(angle), jnp.sin(angle), jnp.broadcast_to(odd * (1.0 / TOTAL), (ROWS, WIDE)))
        for k, table in enumerate(tables):
            for half in range(2):
                turn[k, half * ROWS : (half + 1) * ROWS] = table

        def clear(ch, carry):
            xhi[ch, :, 256:] = jnp.zeros((2 * ITEMS, 128), BF16)
            xlo[ch, :, 256:] = jnp.zeros((2 * ITEMS, 128), BF16)
            return carry

        lax.fori_loop(0, CHUNKS, clear, 0)

    pl.semaphore_wait(barrier, RING + 1)

    lane = lax.broadcasted_iota(jnp.int32, (ITEMS, 128), 1)

    def send_lon(kind, first, last):
        edges = jnp.zeros((ITEMS, 128), F32)
        for i in range(PAIRS):
            edges = jnp.where(lane == i, first(i), edges)
            edges = jnp.where(lane == PAIRS + i, last(i), edges)
        lon_out[kind] = edges
        for side, step in ((0, 1), (1, RING - 1)):
            lon_copy(kind, side, step).start()

    def lon_copy(kind, side, step):
        return pltpu.make_async_remote_copy(
            src_ref=lon_out.at[kind], dst_ref=lon_in.at[kind, side],
            send_sem=lon_sem.at[kind, side], recv_sem=lonr_sem.at[kind, side],
            device_id=(z, (p + step) % RING), device_id_type=MESH,
        )

    def lat_copy(kind, side, step):
        return pltpu.make_async_remote_copy(
            src_ref=lat_out.at[kind, side], dst_ref=lat_in.at[kind, side],
            send_sem=lat_sem.at[kind, side], recv_sem=latr_sem.at[kind, side],
            device_id=((z + step) % BANDS, p), device_id_type=MESH,
        )

    def wait_edges(kind):
        for side, step in ((0, 1), (1, RING - 1)):
            lon_copy(kind, side, step).wait()
        for side, step in ((0, 1), (1, BANDS - 1)):
            lat_copy(kind, side, step).wait()

    def with_edges(kind, i, tile):
        left = lon_in[kind, 0, :, PAIRS + i : PAIRS + i + 1]
        right = lon_in[kind, 1, :, i : i + 1]
        return jnp.where(lane == COLS - 256, right, jnp.where(lane == 127, left, tile))

    loads[0].wait()
    loads[1].wait()

    def flux_first(i):
        return (th[2 * i : 2 * i + 2, :, 0:128] * w[0, 2 * i : 2 * i + 2, :, 0:128]).reshape(ITEMS, 128)[:, 0:1]

    def flux_last(i):
        tile = th[2 * i : 2 * i + 2, :, 256:COLS] * w[0, 2 * i : 2 * i + 2, :, 256:COLS]
        return tile.reshape(ITEMS, COLS - 256)[:, COLS - 257 : COLS - 256]

    send_lon(0, flux_first, flux_last)
    loads[2].wait()
    for side, row in ((0, ROWS - 1), (1, 0)):
        for lev in range(LEVELS):
            lat_out[0, side, lev : lev + 1, 0:COLS] = (
                th[lev, row : row + 1] * w[1, lev, row : row + 1] * geo[0, row : row + 1, 0:COLS]
            )
        lat_copy(0, side, (1, BANDS - 1)[side]).start()

    def shrink(ch, values):
        for half in range(2):
            high, low = split(values * turn[half, :, 0:COLS])
            xhi[ch, half * ITEMS : (half + 1) * ITEMS, 0:COLS] = high
            xlo[ch, half * ITEMS : (half + 1) * ITEMS, 0:COLS] = low
        both = dot(shrink_ref[...], xhi[ch], ((1,), (1,)))
        rest = dot(shrink_ref[0:32], xlo[ch], ((1,), (1,)))
        u[ch] = both[0:RANK] + both[RANK : 2 * RANK] + rest[0:RANK]

    def u_copy(phase, t):
        q = (t + p) % PAIRS
        ch = phase * PAIRS + q
        to = worker(phase, q)
        remote = pltpu.make_async_remote_copy(
            src_ref=u.at[ch], dst_ref=zin.at[p], send_sem=u_sem, recv_sem=z_sem,
            device_id=(z, to), device_id_type=MESH,
        )
        return to, remote, pltpu.make_async_copy(u.at[ch], zin.at[p], z_sem)

    def send_u(phase):
        for t in range(PAIRS):
            to, remote, own = u_copy(phase, t)

            @pl.when(to != p)
            def _():
                remote.start()

            @pl.when(to == p)
            def _():
                own.start()

    @pl.when(polar)
    def _():
        for phase in range(2):

            def step(i, carry):
                shrink(phase * PAIRS + i, w[phase, pl.ds(2 * i, 2)].reshape(ITEMS, COLS))
                return carry

            lax.fori_loop(0, PAIRS, step, 0)
            send_u(phase)

    wait_edges(0)
    row_index = lax.broadcasted_iota(jnp.int32, (ROWS, WIDE), 0)
    for i in range(PAIRS):
        pair = slice(2 * i, 2 * i + 2)
        wide[:, 0:COLS] = (th[pair] * w[0, pair]).reshape(ITEMS, COLS)
        flux = jnp.concatenate([wide[:, 0:256], with_edges(0, i, wide[:, 256:WIDE])], axis=1)
        lon_diff = pltpu.roll(flux, WIDE - 1, 1) - pltpu.roll(flux, 1, 1)
        wide[:, 0:COLS] = (th[pair] * w[1, pair]).reshape(ITEMS, COLS)
        flux = wide[...] * geo[0]
        for k in range(2):
            lev = 2 * i + k
            cells = flux[k * ROWS : (k + 1) * ROWS]
            south = jnp.where(z == 0, 0.0, lat_in[0, 0, lev : lev + 1])
            north = jnp.where(z == BANDS - 1, 0.0, lat_in[0, 1, lev : lev + 1])
            up = jnp.where(row_index == ROWS - 1, north, pltpu.roll(cells, ROWS - 1, 0))
            down = jnp.where(row_index == 0, south, pltpu.roll(cells, 1, 0))
            change = geo[1, 0:ROWS] * (lon_diff[k * ROWS : (k + 1) * ROWS] + (up - down))
            th[lev] = th[lev] - change[:, 0:COLS]

    def local(ch, values):
        high = xhi[ch]
        low = xlo[ch]
        parts = dot(high, near[0], ((1,), (0,))) + dot(low, near[0], ((1,), (0,))) + dot(high, near[1], ((1,), (0,)))
        mixed = turn[1] * parts[0:ITEMS] - turn[0] * parts[ITEMS:]
        return mixed[:, 0:COLS] + turn[2, :, 0:COLS] * values

    def local_wind(phase):
        def step(i, carry):
            pair = pl.ds(2 * i, 2)
            result = local(phase * PAIRS + i, w[phase, pair].reshape(ITEMS, COLS))
            w[phase, pair] = result.reshape(2, ROWS, COLS)
            return carry

        lax.fori_loop(0, PAIRS, step, 0)

    def grown(ch):
        pltpu.make_async_copy(vr.at[ch], vr.at[ch], vr_sem.at[ch]).wait()
        values = vr[ch]
        high = values.astype(BF16).astype(F32)
        stack = jnp.concatenate([high, values - high, high, jnp.zeros((8, 2 * ITEMS), F32)], axis=0).astype(BF16)
        parts = dot(stack, grow_ref[...], ((0,), (0,)))
        mixed = turn[1] * parts[0:ITEMS] - turn[0] * parts[ITEMS:]
        return mixed[:, 0:COLS].reshape(2, ROWS, COLS)

    x = p // 8
    y = (p // 2) % 4
    core = p % 2
    parity = (x + y) % 2
    busy = polar & ((core == 0) | (parity == 0))
    mine = (2 * core + parity) * PAIRS + 2 * x + y // 2

    def v_copy(to):
        remote = pltpu.make_async_remote_copy(
            src_ref=vs.at[to], dst_ref=vr.at[mine], send_sem=v_sem, recv_sem=vr_sem.at[mine],
            device_id=(z, to), device_id_type=MESH,
        )
        return remote, pltpu.make_async_copy(vs.at[to], vr.at[mine], vr_sem.at[mine])

    @pl.when(polar)
    def _():
        def step(i, carry):
            shrink(2 * PAIRS + i, th[pl.ds(2 * i, 2)].reshape(ITEMS, COLS))
            return carry

        lax.fori_loop(0, PAIRS, step, 0)
        send_u(2)
        loads[3].wait()
        loads[4].wait()
        local_wind(0)

    @pl.when(busy)
    def _():
        pltpu.make_async_copy(zin, zin, z_sem).wait()
        high, low = split(zin[...].reshape(RING * RANK, 2 * ITEMS))
        zhi[...] = high
        zlo[...] = low
        part = RING * RANK // 4

        def step(m, carry):
            group = (x + m) % 4
            rows = pl.ds(pl.multiple_of(group * part, part), part)
            result = (
                dot(cross[0, rows], zhi[...], ((1,), (0,)))
                + dot(cross[0, rows], zlo[...], ((1,), (0,)))
                + dot(cross[1, rows], zhi[...], ((1,), (0,)))
            )
            vs[pl.ds(group * 8, 8)] = result.reshape(8, RANK, 2 * ITEMS)
            for j in range(8):
                to = group * 8 + (p + j) % 8
                remote, own = v_copy(to)

                @pl.when(to != p)
                def _():
                    remote.start()

                @pl.when(to == p)
                def _():
                    own.start()

            return carry

        lax.fori_loop(0, 4, step, 0)

    @pl.when(polar)
    def _():
        local_wind(1)

        def local_thick(i, carry):
            pair = pl.ds(2 * i, 2)
            th[pair] = local(2 * PAIRS + i, th[pair].reshape(ITEMS, COLS)).reshape(2, ROWS, COLS)
            return carry

        lax.fori_loop(0, PAIRS, local_thick, 0)

        def step(i, carry):
            pair = pl.ds(2 * i, 2)
            ext[pair, 0:ROWS, 0:COLS] = th[pair] + grown(2 * PAIRS + i)
            return carry

        lax.fori_loop(0, PAIRS, step, 0)

    @pl.when(jnp.logical_not(polar))
    def _():
        ext[:, 0:ROWS, 0:COLS] = th[...]

    def thick_first(i):
        return ext[2 * i : 2 * i + 2, 0:ROWS, 0:128].reshape(ITEMS, 128)[:, 0:1]

    def thick_last(i):
        return ext[2 * i : 2 * i + 2, 0:ROWS, 256:WIDE].reshape(ITEMS, 128)[:, COLS - 257 : COLS - 256]

    for side, row in ((0, ROWS - 1), (1, 0)):
        for lev in range(LEVELS):
            lat_out[1, side, lev : lev + 1, 0:COLS] = ext[lev, row : row + 1, 0:COLS]
        lat_copy(1, side, (1, BANDS - 1)[side]).start()
    send_lon(1, thick_first, thick_last)

    @pl.when(polar)
    def _():
        for phase in range(2):

            def step(i, carry):
                pair = pl.ds(2 * i, 2)
                w[phase, pair] = w[phase, pair] + grown(phase * PAIRS + i)
                return carry

            lax.fori_loop(0, PAIRS, step, 0)

    out_copy = pltpu.make_async_copy(w, out_hbm, done_sem.at[0])
    out_copy.start()

    wait_edges(1)
    for i in range(PAIRS):
        pair = slice(2 * i, 2 * i + 2)
        tile = ext[pair, 0:ROWS, 256:WIDE].reshape(ITEMS, 128)
        ext[pair, 0:ROWS, 256:WIDE] = with_edges(1, i, tile).reshape(2, ROWS, 128)
    for lev in range(LEVELS):
        ext[lev, ROWS : ROWS + 1] = jnp.where(z == BANDS - 1, 0.0, lat_in[1, 1, lev : lev + 1])
        ext[lev, ROWS + 7 : ROWS + 8] = jnp.where(z == 0, 0.0, lat_in[1, 0, lev : lev + 1])
    ext_copy = pltpu.make_async_copy(ext, ext_hbm, done_sem.at[1])
    ext_copy.start()

    @pl.when(polar)
    def _():
        for phase in range(3):
            for t in range(PAIRS):
                to, remote, own = u_copy(phase, t)

                @pl.when(to != p)
                def _():
                    remote.wait_send()

    @pl.when(busy)
    def _():
        def step(i, carry):
            remote, own = v_copy((p + i) % RING)
            remote.wait_send()
            return carry

        lax.fori_loop(1, RING, step, 0)

    @pl.when(jnp.logical_not(polar))
    def _():
        loads[3].wait()
        loads[4].wait()

    out_copy.wait()
    ext_copy.wait()


def gradient_kernel(ext_ref, wind_ref, thick_ref, out_ref):
    z, _ = place()
    _, metric = latitude_tables(z, (ROWS, WIDE))
    cells = ext_ref[0]
    lon_diff = (pltpu.roll(cells, WIDE - 1, 1) - pltpu.roll(cells, 1, 1))[0:ROWS]
    lat_diff = (pltpu.roll(cells, ROWS + 7, 0) - pltpu.roll(cells, 1, 0))[0:ROWS]
    thick_ref[0] = cells[0:ROWS, 0:COLS]
    out_ref[0, 0] = wind_ref[0, 0] - (press_coef * metric * lon_diff)[:, 0:COLS]
    out_ref[1, 0] = wind_ref[1, 0] - (press_coef * lat_diff)[:, 0:COLS]


def body(thickness, wind, cutoff, tables):
    shrink, grow, near, cross = tables
    any_space = pl.BlockSpec(memory_space=pl.ANY)
    vmem = pl.BlockSpec(memory_space=pltpu.VMEM)
    dma = pltpu.SemaphoreType.DMA
    ext, moved = pl.pallas_call(
        far_kernel,
        out_shape=(
            jax.ShapeDtypeStruct((LEVELS, ROWS + 8, WIDE), F32),
            jax.ShapeDtypeStruct((2, LEVELS, ROWS, COLS), F32),
        ),
        in_specs=[vmem, vmem, vmem, any_space, any_space, any_space, any_space],
        out_specs=(any_space, any_space),
        scratch_shapes=[
            pltpu.VMEM((LEVELS, ROWS, COLS), F32),
            pltpu.VMEM((2, LEVELS, ROWS, COLS), F32),
            pltpu.VMEM((LEVELS, ROWS + 8, WIDE), F32),
            pltpu.VMEM((CHUNKS, 2 * ITEMS, WIDE), BF16),
            pltpu.VMEM((CHUNKS, 2 * ITEMS, WIDE), BF16),
            pltpu.VMEM((3, ITEMS, WIDE), F32),
            pltpu.VMEM((2, ITEMS, WIDE), F32),
            pltpu.VMEM((ITEMS, WIDE), F32),
            pltpu.VMEM((2, WIDE, WIDE), BF16),
            pltpu.VMEM((2, RING * RANK, RING * RANK), BF16),
            pltpu.VMEM((CHUNKS, RANK, 2 * ITEMS), F32),
            pltpu.VMEM((RING, RANK, 2 * ITEMS), F32),
            pltpu.VMEM((RING, RANK, 2 * ITEMS), F32),
            pltpu.VMEM((CHUNKS, RANK, 2 * ITEMS), F32),
            pltpu.VMEM((RING * RANK, 2 * ITEMS), BF16),
            pltpu.VMEM((RING * RANK, 2 * ITEMS), BF16),
            pltpu.VMEM((2, ITEMS, 128), F32),
            pltpu.VMEM((2, 2, ITEMS, 128), F32),
            pltpu.VMEM((2, 2, LEVELS, WIDE), F32),
            pltpu.VMEM((2, 2, LEVELS, WIDE), F32),
            dma((5,)),
            dma,
            dma,
            dma,
            dma((CHUNKS,)),
            dma((2, 2)),
            dma((2, 2)),
            dma((2, 2)),
            dma((2, 2)),
            dma((2,)),
        ],
        compiler_params=pltpu.CompilerParams(
            collective_id=0, has_side_effects=True, vmem_limit_bytes=48 * 2**20
        ),
        name="far",
    )(cutoff.reshape(1, -1), shrink, grow, thickness, wind, near, cross)
    return pl.pallas_call(
        gradient_kernel,
        grid=(LEVELS,),
        out_shape=(
            jax.ShapeDtypeStruct((LEVELS, ROWS, COLS), F32),
            jax.ShapeDtypeStruct((2, LEVELS, ROWS, COLS), F32),
        ),
        in_specs=[
            pl.BlockSpec((1, ROWS + 8, WIDE), lambda i: (i, 0, 0)),
            pl.BlockSpec((2, 1, ROWS, COLS), lambda i: (0, i, 0, 0)),
        ],
        out_specs=(
            pl.BlockSpec((1, ROWS, COLS), lambda i: (i, 0, 0)),
            pl.BlockSpec((2, 1, ROWS, COLS), lambda i: (0, i, 0, 0)),
        ),
        name="gradient",
    )(ext, moved)


def solution(mesh):
    near, basis, cross = cauchy_tables()
    pad = WIDE - COLS
    near = jnp.stack(two_parts(np.pad(near.T, ((0, pad), (0, pad)))))
    cross = jnp.stack(two_parts(cross))
    high, low = two_parts(np.pad(basis.T, ((0, 0), (0, pad))))
    shrink = jnp.concatenate([high, low])
    grow = jnp.concatenate([high, high, low, jnp.zeros((8, WIDE), BF16)])
    in_specs = (P(None, "lat", "lon"), P(None, None, "lat", "lon"), P())
    out_specs = (P(None, "lat", "lon"), P(None, None, "lat", "lon"))

    def step(thickness, wind, cutoff):
        return body(thickness, wind, cutoff, (shrink, grow, near, cross))

    return jax.shard_map(step, mesh=mesh, in_specs=in_specs, out_specs=out_specs, check_vma=False)
```

time: 133 us -> 62.3 us (0.47)
  the two profiles are of different devices: /device:TPU:96 before, /device:TPU:1 now
where the time goes in v1:
time: 62.3 us; the launch traced here: 61.8 us
  Pallas kernels  55.1 us (88%)
  local copies, waits for them, and re-layouts  5.96 us (10%)
  between operations  0.66 us (1%)
    pallas_call x1, Pallas kernels, body(): pl.pallas_call(far_kernel, out_shape=(jax.ShapeDtypeStruct((LEVELS, ROWS...  43.7 us
    pallas_call x1, Pallas kernels, body(): pl.pallas_call(gradient_kernel, grid=(LEVELS,), out_shape=(jax.ShapeDtype...  11.5 us
    unnamed x12, local copies, waits for them, and re-layouts  5.96 us

profile of v1, /device:TPU:1, one launch (start us, length us, event | category | flops | bytes accessed | tf_op | source)
XLA Modules:
  0.0 61.8 jit_solution(11183398331476483048)
XLA Ops:
  0.6 0.0 copy-start.1
  0.6 1.4 %copy-done.1 = f32[16,64,360]{2,1,0:T(8,128)S(1)} copy-done((f32[16,64,360]{2,1,0:T(8,128)S(1)}, f32[16,64,360]{2,1,0:T(8,128)}, u32[]{:S(2)}) %copy-start.1) | copy-done | bytes 1474584
  2.0 0.0 copy-start.2
  2.0 1.1 %copy-done.2 = bf16[2,384,384]{2,1,0:T(8,128)(2,1)S(1)} copy-done((bf16[2,384,384]{2,1,0:T(8,128)(2,1)S(1)}, bf16[2,384,384]{2,1,0:T(8,128)(2,1)}, u32[]{:S(2)}) %copy-start.2) | copy-done | bytes 589848
  3.1 0.0 copy-start.3
  3.1 0.8 %copy-done.3 = bf16[80,384]{1,0:T(8,128)(2,1)S(1)} copy-done((bf16[80,384]{1,0:T(8,128)(2,1)S(1)}, bf16[80,384]{1,0:T(8,128)(2,1)}, u32[]{:S(2)}) %copy-start.3) | copy-done | bytes 61464
  3.9 0.0 copy-start.4
  3.9 0.8 %copy-done.4 = bf16[48,384]{1,0:T(8,128)(2,1)S(1)} copy-done((bf16[48,384]{1,0:T(8,128)(2,1)S(1)}, bf16[48,384]{1,0:T(8,128)(2,1)}, u32[]{:S(2)}) %copy-start.4) | copy-done | bytes 36888
  4.7 0.0 copy-start.5
  4.7 0.7 %copy-done.5 = s32[256]{0:T(256)S(1)} copy-done((s32[256]{0:T(256)S(1)}, s32[256]{0:T(256)}, u32[]{:S(2)}) %copy-start.5) | copy-done | bytes 1048
  5.4 43.7 %far.1 = (f32[16,72,384]{2,1,0:T(8,128)S(1)}, f32[2,16,64,360]{3,2,1,0:T(8,128)}) custom-call(s32[1,256]{1,0:T(1,128)S(1)} %bitcast.1, bf16[48,384]{1,0:T(8,128)(2,1)S(1)} %copy-done.4, bf16[80,384]{1,0:T(8,128)(2,1)S(1)} %copy-done.3, f32[16,64,360]{2,1,0:T(8,128)S(1)} %copy-done.1, f32[2,16,64,360]{3,2,1,0:T(8,128)} %wind_hbm.1, ...), custom_call_target="tpu_custom_call" | custom-call | tf_op jit(solution)/shard_map/far/pallas_call | solution.py:447
  49.0 0.0 copy-start
  49.1 1.2 %copy-done = f32[16,72,384]{2,1,0:T(8,128)} copy-done((f32[16,72,384]{2,1,0:T(8,128)}, f32[16,72,384]{2,1,0:T(8,128)S(1)}, u32[]{:S(2)}) %copy-start) | copy-done | bytes 1769496
  50.3 11.5 %gradient.1 = (f32[16,64,360]{2,1,0:T(8,128)}, f32[2,16,64,360]{3,2,1,0:T(8,128)}) custom-call(f32[16,72,384]{2,1,0:T(8,128)} %copy-done, f32[2,16,64,360]{3,2,1,0:T(8,128)} %get-tuple-element.5.wind_ref), custom_call_target="tpu_custom_call" | custom-call | tf_op jit(solution)/shard_map/gradient/pallas_call | solution.py:492
Async XLA Ops:
  0.6 1.4 %copy-start.1 = (f32[16,64,360]{2,1,0:T(8,128)S(1)}, f32[16,64,360]{2,1,0:T(8,128)}, u32[]{:S(2)}) copy-start(f32[16,64,360]{2,1,0:T(8,128)} %th_hbm.1) | copy-start | bytes 4423684
  2.0 1.1 %copy-start.2 = (bf16[2,384,384]{2,1,0:T(8,128)(2,1)S(1)}, bf16[2,384,384]{2,1,0:T(8,128)(2,1)}, u32[]{:S(2)}) copy-start(bf16[2,384,384]{2,1,0:T(8,128)(2,1)} %constant.10.clone.near_hbm) | copy-start | bytes 1769476
  3.1 0.8 %copy-start.3 = (bf16[80,384]{1,0:T(8,128)(2,1)S(1)}, bf16[80,384]{1,0:T(8,128)(2,1)}, u32[]{:S(2)}) copy-start(bf16[80,384]{1,0:T(8,128)(2,1)} %constant.9.clone.grow_ref) | copy-start | bytes 184324
  3.9 0.8 %copy-start.4 = (bf16[48,384]{1,0:T(8,128)(2,1)S(1)}, bf16[48,384]{1,0:T(8,128)(2,1)}, u32[]{:S(2)}) copy-start(bf16[48,384]{1,0:T(8,128)(2,1)} %constant.8.clone.shrink_ref) | copy-start | bytes 110596
  4.7 0.7 %copy-start.5 = (s32[256]{0:T(256)S(1)}, s32[256]{0:T(256)}, u32[]{:S(2)}) copy-start(s32[256]{0:T(256)} %param.9) | copy-start | bytes 3076
  49.0 1.2 %copy-start = (f32[16,72,384]{2,1,0:T(8,128)}, f32[16,72,384]{2,1,0:T(8,128)S(1)}, u32[]{:S(2)}) copy-start(f32[16,72,384]{2,1,0:T(8,128)S(1)} %get-tuple-element.4.ext_ref) | copy-start | bytes 5308420

commit v2 on v1

--- a/solution.py
+++ b/solution.py
@@ -15,7 +15,13 @@
 
 advect_coef = 0.05
 press_coef = 0.1
-RANK = 24
+FAR = 8
+NEAR = 16
+SUB = 128
+SUB_RANKS = (13, 22, 13)
+INNER = sum(SUB_RANKS)
+SHORT = FAR + 2 * NEAR + INNER
+SPREAD = INNER + 2 * NEAR
 LEVELS = 16
 ROWS = 64
 COLS = 360
@@ -25,25 +31,66 @@
 TOTAL = COLS * RING
 PAIRS = LEVELS // 2
 CHUNKS = 3 * PAIRS
+STEP = 4
 ITEMS = 2 * ROWS
+
+
+def kernel_block(targets, sources):
+    return 1.0 / (TOTAL * np.sin(np.pi * (targets[:, None] - sources[None]) / TOTAL))
 
 
 def cauchy_tables():
     inside = np.arange(COLS)
-    outside = np.arange(COLS, TOTAL)
-    far = 1.0 / (TOTAL * np.sin(np.pi * (inside[:, None] - outside[None]) / TOTAL))
-    basis = np.linalg.svd(far, full_matrices=False)[0][:, :RANK]
-    gap = inside[:, None] - inside[None]
-    near = np.where(gap == 0, 0.0, 1.0 / (TOTAL * np.sin(np.pi * gap / TOTAL) + (gap == 0)))
-    cross = np.zeros((RING, RANK, RING, RANK))
-    for shift in range(1 - RING, RING):
-        if shift == 0:
-            continue
-        piece = basis.T @ (1.0 / (TOTAL * np.sin(np.pi * (gap + shift * COLS) / TOTAL))) @ basis
-        for p in range(RING):
-            if 0 <= p - shift < RING:
-                cross[p, :, p - shift, :] = piece
-    return near, basis, cross.reshape(RING * RANK, RING * RANK)
+    gap = np.arange(SUB)[:, None] - np.arange(SUB)[None]
+    diagonal = np.where(gap == 0, 0.0, 1.0 / (TOTAL * np.sin(np.pi * gap / TOTAL) + (gap == 0)))
+    far = np.linalg.svd(kernel_block(inside, np.arange(2 * COLS, TOTAL - COLS)), full_matrices=False)[0][:, :FAR]
+    cross = np.zeros((RING, FAR, RING, FAR))
+    for p in range(RING):
+        for q in range(RING):
+            if min((p - q) % RING, (q - p) % RING) >= 2:
+                cross[p, :, q, :] = far.T @ kernel_block(p * COLS + inside, q * COLS + inside) @ far
+    left, scale, right = np.linalg.svd(kernel_block(COLS + inside, inside))
+    shorten = [far.T, right[:NEAR], left[:, :NEAR].T]
+    from_left = (left * scale)[:, :NEAR].T
+    from_right = -(scale[:, None] * right)[:NEAR]
+    spread = []
+    for k, rank in enumerate(SUB_RANKS):
+        own = inside[k * SUB : (k + 1) * SUB]
+        other = np.setdiff1d(inside, own)
+        rows = np.linalg.svd(kernel_block(other, own), full_matrices=False)[2][:rank]
+        padded = np.zeros((rank, COLS))
+        padded[:, own] = rows
+        shorten.append(padded)
+        padded = np.zeros((rank, COLS))
+        padded[:, other] = (kernel_block(other, own) @ rows.T).T
+        spread.append(padded)
+    spread += [from_left, from_right]
+    return diagonal, np.concatenate(shorten), np.concatenate(spread), far.T, cross.reshape(RING * FAR, RING * FAR)
+
+
+def widened(table):
+    return np.pad(table, ((0, 0), (0, WIDE - COLS)))
+
+
+def all_tables():
+    diagonal, shorten, spread, far, cross = cauchy_tables()
+    high, low = two_parts(diagonal.T)
+    near = np.block([[high, low], [high, np.zeros_like(low)]])
+    high, low = two_parts(widened(shorten))
+    zero = np.zeros((SHORT, SUB), BF16)
+    first = [high[:, k : k + SUB] for k in (0, SUB, 2 * SUB)]
+    second = [low[:, k : k + SUB] for k in (0, SUB, 2 * SUB)]
+    short = np.concatenate(
+        [
+            np.concatenate([part for f in first for part in (f, f)], axis=1),
+            np.concatenate([part for f in second for part in (f, zero)], axis=1),
+        ]
+    )
+    high, low = two_parts(widened(spread))
+    early = np.concatenate([high, high, low])
+    high, low = two_parts(widened(far))
+    late = np.concatenate([high, high, low, np.zeros((FAR, WIDE), BF16)])
+    return [jnp.asarray(t) for t in (near, short, early, late, np.stack(two_parts(cross)))]
 
 
 def two_parts(table):
@@ -82,11 +129,12 @@
 
 
 def far_kernel(
-    cut_ref, shrink_ref, grow_ref, th_hbm, wind_hbm, near_hbm, cross_hbm,
+    cut_hbm, th_hbm, wind_hbm, near_hbm, short_hbm, early_hbm, late_hbm, cross_hbm,
     ext_hbm, out_hbm,
-    th, w, ext, xhi, xlo, turn, geo, wide, near, cross, u, zin, vs, vr, zhi, zlo,
+    cut_ref, th, w, ext, xs, turn, geo, wide, near, short, early, late, cross,
+    inner, to_near, from_near, u, zin, vs, vr,
     lon_out, lon_in, lat_out, lat_in,
-    load_sem, u_sem, z_sem, v_sem, vr_sem, lon_sem, lonr_sem, lat_sem, latr_sem, done_sem,
+    load_sem, near_sem, nearr_sem, u_sem, z_sem, v_sem, vr_sem, lon_sem, lonr_sem, lat_sem, latr_sem, done_sem,
 ):
     z, p = place()
     polar = (z < 2) | (z >= 6)
@@ -94,11 +142,15 @@
         pltpu.make_async_copy(wind_hbm.at[0], w.at[0], load_sem.at[0]),
         pltpu.make_async_copy(th_hbm, th, load_sem.at[1]),
         pltpu.make_async_copy(wind_hbm.at[1], w.at[1], load_sem.at[2]),
-        pltpu.make_async_copy(near_hbm, near, load_sem.at[3]),
-        pltpu.make_async_copy(cross_hbm, cross, load_sem.at[4]),
+        pltpu.make_async_copy(cut_hbm, cut_ref, load_sem.at[3]),
+        pltpu.make_async_copy(short_hbm, short, load_sem.at[4]),
+        pltpu.make_async_copy(near_hbm, near, load_sem.at[5]),
+        pltpu.make_async_copy(early_hbm, early, load_sem.at[6]),
+        pltpu.make_async_copy(cross_hbm, cross, load_sem.at[7]),
+        pltpu.make_async_copy(late_hbm, late, load_sem.at[8]),
     ]
-    for copy in loads:
-        copy.start()
+    for k in (3, 0, 1, 2, 4, 5, 6, 7, 8):
+        loads[k].start()
     barrier = pltpu.get_barrier_semaphore()
 
     def greet(i, carry):
@@ -114,6 +166,8 @@
         geo[0, half * ROWS : (half + 1) * ROWS] = cosine
         geo[1, half * ROWS : (half + 1) * ROWS] = advect_coef * metric
     wide[...] = jnp.zeros((ITEMS, WIDE), F32)
+
+    loads[3].wait()
 
     @pl.when(polar)
     def _():
@@ -133,8 +187,7 @@
                 turn[k, half * ROWS : (half + 1) * ROWS] = table
 
         def clear(ch, carry):
-            xhi[ch, :, 256:] = jnp.zeros((2 * ITEMS, 128), BF16)
-            xlo[ch, :, 256:] = jnp.zeros((2 * ITEMS, 128), BF16)
+            xs[ch, :, 4 * SUB :] = jnp.zeros((2 * ITEMS, 2 * SUB), BF16)
             return carry
 
         lax.fori_loop(0, CHUNKS, clear, 0)
@@ -198,12 +251,26 @@
 
     def shrink(ch, values):
         for half in range(2):
+            rows = slice(half * ITEMS, (half + 1) * ITEMS)
             high, low = split(values * turn[half, :, 0:COLS])
-            xhi[ch, half * ITEMS : (half + 1) * ITEMS, 0:COLS] = high
-            xlo[ch, half * ITEMS : (half + 1) * ITEMS, 0:COLS] = low
-        both = dot(shrink_ref[...], xhi[ch], ((1,), (1,)))
-        rest = dot(shrink_ref[0:32], xlo[ch], ((1,), (1,)))
-        u[ch] = both[0:RANK] + both[RANK : 2 * RANK] + rest[0:RANK]
+            for k in range(3):
+                size = min(SUB, COLS - k * SUB)
+                xs[ch, rows, 2 * k * SUB : 2 * k * SUB + size] = high[:, k * SUB : k * SUB + size]
+                xs[ch, rows, (2 * k + 1) * SUB : (2 * k + 1) * SUB + size] = low[:, k * SUB : k * SUB + size]
+        both = dot(short[...], xs[ch], ((1,), (1,)))
+        both = both[0:SHORT] + both[SHORT:]
+        u[ch] = both[0:FAR]
+        to_near[0, ch] = both[FAR : FAR + NEAR]
+        to_near[1, ch] = both[FAR + NEAR : FAR + 2 * NEAR]
+        inner[ch] = both[FAR + 2 * NEAR :]
+
+    def near_copy(phase, side):
+        part = pl.ds(phase * PAIRS, PAIRS)
+        return pltpu.make_async_remote_copy(
+            src_ref=to_near.at[side, part], dst_ref=from_near.at[side, part],
+            send_sem=near_sem.at[phase, side], recv_sem=nearr_sem.at[phase, side],
+            device_id=(z, (p + (1, RING - 1)[side]) % RING), device_id_type=MESH,
+        )
 
     def u_copy(phase, t):
         q = (t + p) % PAIRS
@@ -229,6 +296,7 @@
 
     @pl.when(polar)
     def _():
+        loads[4].wait()
         for phase in range(2):
 
             def step(i, carry):
@@ -237,6 +305,8 @@
 
             lax.fori_loop(0, PAIRS, step, 0)
             send_u(phase)
+            for side in range(2):
+                near_copy(phase, side).start()
 
     wait_edges(0)
     row_index = lax.broadcasted_iota(jnp.int32, (ROWS, WIDE), 0)
@@ -257,14 +327,28 @@
             change = geo[1, 0:ROWS] * (lon_diff[k * ROWS : (k + 1) * ROWS] + (up - down))
             th[lev] = th[lev] - change[:, 0:COLS]
 
+    first_sign = jnp.where(p == 0, -1.0, 1.0).astype(F32)
+    last_sign = jnp.where(p == RING - 1, -1.0, 1.0).astype(F32)
+
+    def turned_back(parts):
+        mixed = turn[1] * parts[0:ITEMS] - turn[0] * parts[ITEMS:]
+        return mixed[:, 0:COLS]
+
     def local(ch, values):
-        high = xhi[ch]
-        low = xlo[ch]
-        parts = dot(high, near[0], ((1,), (0,))) + dot(low, near[0], ((1,), (0,))) + dot(high, near[1], ((1,), (0,)))
-        mixed = turn[1] * parts[0:ITEMS] - turn[0] * parts[ITEMS:]
-        return mixed[:, 0:COLS] + turn[2, :, 0:COLS] * values
+        pieces = []
+        for k in range(3):
+            both = dot(xs[ch, :, 2 * k * SUB : (2 * k + 2) * SUB], near[...], ((1,), (0,)))
+            pieces.append(both[:, 0:SUB] + both[:, SUB:])
+        stack = jnp.concatenate([inner[ch], first_sign * from_near[0, ch], last_sign * from_near[1, ch]], axis=0)
+        high = stack.astype(BF16).astype(F32)
+        stack = jnp.concatenate([high, stack - high, high], axis=0).astype(BF16)
+        parts = jnp.concatenate(pieces, axis=1) + dot(stack, early[...], ((0,), (0,)))
+        return turned_back(parts) + turn[2, :, 0:COLS] * values
 
     def local_wind(phase):
+        for side in range(2):
+            near_copy(phase, side).wait()
+
         def step(i, carry):
             pair = pl.ds(2 * i, 2)
             result = local(phase * PAIRS + i, w[phase, pair].reshape(ITEMS, COLS))
@@ -277,10 +361,8 @@
         pltpu.make_async_copy(vr.at[ch], vr.at[ch], vr_sem.at[ch]).wait()
         values = vr[ch]
         high = values.astype(BF16).astype(F32)
-        stack = jnp.concatenate([high, values - high, high, jnp.zeros((8, 2 * ITEMS), F32)], axis=0).astype(BF16)
-        parts = dot(stack, grow_ref[...], ((0,), (0,)))
-        mixed = turn[1] * parts[0:ITEMS] - turn[0] * parts[ITEMS:]
-        return mixed[:, 0:COLS].reshape(2, ROWS, COLS)
+        stack = jnp.concatenate([high, values - high, high, jnp.zeros((FAR, 2 * ITEMS), F32)], axis=0).astype(BF16)
+        return turned_back(dot(stack, late[...], ((0,), (0,)))).reshape(2, ROWS, COLS)
 
     x = p // 8
     y = (p // 2) % 4
@@ -304,46 +386,37 @@
 
         lax.fori_loop(0, PAIRS, step, 0)
         send_u(2)
-        loads[3].wait()
-        loads[4].wait()
+        for side in range(2):
+            near_copy(2, side).start()
+        for k in range(5, 9):
+            loads[k].wait()
         local_wind(0)
 
     @pl.when(busy)
     def _():
         pltpu.make_async_copy(zin, zin, z_sem).wait()
-        high, low = split(zin[...].reshape(RING * RANK, 2 * ITEMS))
-        zhi[...] = high
-        zlo[...] = low
-        part = RING * RANK // 4
-
-        def step(m, carry):
-            group = (x + m) % 4
-            rows = pl.ds(pl.multiple_of(group * part, part), part)
-            result = (
-                dot(cross[0, rows], zhi[...], ((1,), (0,)))
-                + dot(cross[0, rows], zlo[...], ((1,), (0,)))
-                + dot(cross[1, rows], zhi[...], ((1,), (0,)))
-            )
-            vs[pl.ds(group * 8, 8)] = result.reshape(8, RANK, 2 * ITEMS)
-            for j in range(8):
-                to = group * 8 + (p + j) % 8
-                remote, own = v_copy(to)
-
-                @pl.when(to != p)
-                def _():
-                    remote.start()
-
-                @pl.when(to == p)
-                def _():
-                    own.start()
-
+        high, low = split(zin[...].reshape(RING * FAR, 2 * ITEMS))
+        result = (
+            dot(cross[0], high, ((1,), (0,)))
+            + dot(cross[0], low, ((1,), (0,)))
+            + dot(cross[1], high, ((1,), (0,)))
+        )
+        vs[...] = result.reshape(RING, FAR, 2 * ITEMS)
+        remote, own = v_copy(p)
+        own.start()
+
+        def step(i, carry):
+            remote, own = v_copy((p + i) % RING)
+            remote.start()
             return carry
 
-        lax.fori_loop(0, 4, step, 0)
+        lax.fori_loop(1, RING, step, 0)
 
     @pl.when(polar)
     def _():
         local_wind(1)
+        for side in range(2):
+            near_copy(2, side).wait()
 
         def local_thick(i, carry):
             pair = pl.ds(2 * i, 2)
@@ -421,28 +494,32 @@
 
     @pl.when(jnp.logical_not(polar))
     def _():
-        loads[3].wait()
-        loads[4].wait()
+        for k in range(4, 9):
+            loads[k].wait()
 
     out_copy.wait()
     ext_copy.wait()
 
 
-def gradient_kernel(ext_ref, wind_ref, thick_ref, out_ref):
+def gradient_kernel(ext_ref, wind_ref, thick_ref, out_ref, geo):
     z, _ = place()
-    _, metric = latitude_tables(z, (ROWS, WIDE))
-    cells = ext_ref[0]
-    lon_diff = (pltpu.roll(cells, WIDE - 1, 1) - pltpu.roll(cells, 1, 1))[0:ROWS]
-    lat_diff = (pltpu.roll(cells, ROWS + 7, 0) - pltpu.roll(cells, 1, 0))[0:ROWS]
-    thick_ref[0] = cells[0:ROWS, 0:COLS]
-    out_ref[0, 0] = wind_ref[0, 0] - (press_coef * metric * lon_diff)[:, 0:COLS]
-    out_ref[1, 0] = wind_ref[1, 0] - (press_coef * lat_diff)[:, 0:COLS]
+
+    @pl.when(pl.program_id(0) == 0)
+    def _():
+        geo[...] = press_coef * latitude_tables(z, (ROWS, WIDE))[1]
+
+    for k in range(STEP):
+        cells = ext_ref[k]
+        lon_diff = pltpu.roll(cells, WIDE - 1, 1) - pltpu.roll(cells, 1, 1)
+        lat_diff = pltpu.roll(cells, ROWS + 7, 0) - pltpu.roll(cells, 1, 0)
+        thick_ref[k] = cells[0:ROWS, 0:COLS]
+        out_ref[0, k] = wind_ref[0, k] - (geo[...] * lon_diff[0:ROWS])[:, 0:COLS]
+        out_ref[1, k] = wind_ref[1, k] - (press_coef * lat_diff[0:ROWS])[:, 0:COLS]
 
 
 def body(thickness, wind, cutoff, tables):
-    shrink, grow, near, cross = tables
+    near, short, early, late, cross = tables
     any_space = pl.BlockSpec(memory_space=pl.ANY)
-    vmem = pl.BlockSpec(memory_space=pltpu.VMEM)
     dma = pltpu.SemaphoreType.DMA
     ext, moved = pl.pallas_call(
         far_kernel,
@@ -450,30 +527,36 @@
             jax.ShapeDtypeStruct((LEVELS, ROWS + 8, WIDE), F32),
             jax.ShapeDtypeStruct((2, LEVELS, ROWS, COLS), F32),
         ),
-        in_specs=[vmem, vmem, vmem, any_space, any_space, any_space, any_space],
+        in_specs=[any_space] * 8,
         out_specs=(any_space, any_space),
         scratch_shapes=[
+            pltpu.VMEM((1, 4 * ROWS), jnp.int32),
             pltpu.VMEM((LEVELS, ROWS, COLS), F32),
             pltpu.VMEM((2, LEVELS, ROWS, COLS), F32),
             pltpu.VMEM((LEVELS, ROWS + 8, WIDE), F32),
-            pltpu.VMEM((CHUNKS, 2 * ITEMS, WIDE), BF16),
-            pltpu.VMEM((CHUNKS, 2 * ITEMS, WIDE), BF16),
+            pltpu.VMEM((CHUNKS, 2 * ITEMS, 2 * WIDE), BF16),
             pltpu.VMEM((3, ITEMS, WIDE), F32),
             pltpu.VMEM((2, ITEMS, WIDE), F32),
             pltpu.VMEM((ITEMS, WIDE), F32),
-            pltpu.VMEM((2, WIDE, WIDE), BF16),
-            pltpu.VMEM((2, RING * RANK, RING * RANK), BF16),
-            pltpu.VMEM((CHUNKS, RANK, 2 * ITEMS), F32),
-            pltpu.VMEM((RING, RANK, 2 * ITEMS), F32),
-            pltpu.VMEM((RING, RANK, 2 * ITEMS), F32),
-            pltpu.VMEM((CHUNKS, RANK, 2 * ITEMS), F32),
-            pltpu.VMEM((RING * RANK, 2 * ITEMS), BF16),
-            pltpu.VMEM((RING * RANK, 2 * ITEMS), BF16),
+            pltpu.VMEM(near.shape, BF16),
+            pltpu.VMEM(short.shape, BF16),
+            pltpu.VMEM(early.shape, BF16),
+            pltpu.VMEM(late.shape, BF16),
+            pltpu.VMEM(cross.shape, BF16),
+            pltpu.VMEM((CHUNKS, INNER, 2 * ITEMS), F32),
+            pltpu.VMEM((2, CHUNKS, NEAR, 2 * ITEMS), F32),
+            pltpu.VMEM((2, CHUNKS, NEAR, 2 * ITEMS), F32),
+            pltpu.VMEM((CHUNKS, FAR, 2 * ITEMS), F32),
+            pltpu.VMEM((RING, FAR, 2 * ITEMS), F32),
+            pltpu.VMEM((RING, FAR, 2 * ITEMS), F32),
+            pltpu.VMEM((CHUNKS, FAR, 2 * ITEMS), F32),
             pltpu.VMEM((2, ITEMS, 128), F32),
             pltpu.VMEM((2, 2, ITEMS, 128), F32),
             pltpu.VMEM((2, 2, LEVELS, WIDE), F32),
             pltpu.VMEM((2, 2, LEVELS, WIDE), F32),
-            dma((5,)),
+            dma((9,)),
+            dma((3, 2)),
+            dma((3, 2)),
             dma,
             dma,
             dma,
@@ -485,41 +568,36 @@
             dma((2,)),
         ],
         compiler_params=pltpu.CompilerParams(
-            collective_id=0, has_side_effects=True, vmem_limit_bytes=48 * 2**20
+            collective_id=0, has_side_effects=True, vmem_limit_bytes=60 * 2**20
         ),
         name="far",
-    )(cutoff.reshape(1, -1), shrink, grow, thickness, wind, near, cross)
+    )(cutoff.reshape(1, -1), thickness, wind, near, short, early, late, cross)
     return pl.pallas_call(
         gradient_kernel,
-        grid=(LEVELS,),
+        grid=(LEVELS // STEP,),
         out_shape=(
             jax.ShapeDtypeStruct((LEVELS, ROWS, COLS), F32),
             jax.ShapeDtypeStruct((2, LEVELS, ROWS, COLS), F32),
         ),
         in_specs=[
-            pl.BlockSpec((1, ROWS + 8, WIDE), lambda i: (i, 0, 0)),
-            pl.BlockSpec((2, 1, ROWS, COLS), lambda i: (0, i, 0, 0)),
+            pl.BlockSpec((STEP, ROWS + 8, WIDE), lambda i: (i, 0, 0)),
+            pl.BlockSpec((2, STEP, ROWS, COLS), lambda i: (0, i, 0, 0)),
         ],
         out_specs=(
-            pl.BlockSpec((1, ROWS, COLS), lambda i: (i, 0, 0)),
-            pl.BlockSpec((2, 1, ROWS, COLS), lambda i: (0, i, 0, 0)),
+            pl.BlockSpec((STEP, ROWS, COLS), lambda i: (i, 0, 0)),
+            pl.BlockSpec((2, STEP, ROWS, COLS), lambda i: (0, i, 0, 0)),
         ),
+        scratch_shapes=[pltpu.VMEM((ROWS, WIDE), F32)],
         name="gradient",
     )(ext, moved)
 
 
 def solution(mesh):
-    near, basis, cross = cauchy_tables()
-    pad = WIDE - COLS
-    near = jnp.stack(two_parts(np.pad(near.T, ((0, pad), (0, pad)))))
-    cross = jnp.stack(two_parts(cross))
-    high, low = two_parts(np.pad(basis.T, ((0, 0), (0, pad))))
-    shrink = jnp.concatenate([high, low])
-    grow = jnp.concatenate([high, high, low, jnp.zeros((8, WIDE), BF16)])
+    tables = all_tables()
     in_specs = (P(None, "lat", "lon"), P(None, None, "lat", "lon"), P())
     out_specs = (P(None, "lat", "lon"), P(None, None, "lat", "lon"))
 
     def step(thickness, wind, cutoff):
-        return body(thickness, wind, cutoff, (shrink, grow, near, cross))
+        return body(thickness, wind, cutoff, tables)
 
     return jax.shard_map(step, mesh=mesh, in_specs=in_specs, out_specs=out_specs, check_vma=False)

time: 62.3 us -> 47.4 us (0.76)
  Pallas kernels: 55.1 us -> 46.6 us
  local copies, waits for them, and re-layouts: 5.96 us -> 0 us
    pallas_call x1, Pallas kernels: 11.5 us -> 5.27 us  [body(): pl.pallas_call(gradient_kernel, grid=(LEVELS // STEP,), out_shape=(jax.Sh...]
    unnamed x12 -> x0, local copies, waits for them, and re-layouts: 5.96 us -> none
    pallas_call x1, Pallas kernels: 43.7 us -> 41.3 us  [body(): pl.pallas_call(far_kernel, out_shape=(jax.ShapeDtypeStruct((LEVELS, ROWS...]
where the time goes in v2:
time: 47.4 us; the launch traced here: 47.2 us
  Pallas kernels  46.6 us (98%)
  between operations  0.64 us (1%)
    pallas_call x1, Pallas kernels, body(): pl.pallas_call(far_kernel, out_shape=(jax.ShapeDtypeStruct((LEVELS, ROWS...  41.3 us
    pallas_call x1, Pallas kernels, body(): pl.pallas_call(gradient_kernel, grid=(LEVELS // STEP,), out_shape=(jax.Sh...  5.27 us

profile of v2, /device:TPU:1, one launch (start us, length us, event | category | flops | bytes accessed | tf_op | source)
XLA Modules:
  0.0 47.2 jit_solution(548722183636741898)
XLA Ops:
  0.6 41.3 %far.1 = (f32[16,72,384]{2,1,0:T(8,128)}, f32[2,16,64,360]{3,2,1,0:T(8,128)}) custom-call(s32[1,256]{1,0:T(1,128)} %bitcast.1, f32[16,64,360]{2,1,0:T(8,128)} %th_hbm.1, f32[2,16,64,360]{3,2,1,0:T(8,128)} %wind_hbm.1, bf16[256,256]{1,0:T(8,128)(2,1)} %constant.10.clone.near_hbm, bf16[176,768]{1,0:T(8,128)(2,1)} %constant.11.clone.short_hbm, ...), custom_call_target="tpu_custom_call" | custom-call | tf_op jit(solution)/shard_map/far/pallas_call | solution.py:524
  42.0 5.3 %gradient.1 = (f32[16,64,360]{2,1,0:T(8,128)}, f32[2,16,64,360]{3,2,1,0:T(8,128)}) custom-call(f32[16,72,384]{2,1,0:T(8,128)} %get-tuple-element.4.ext_ref, f32[2,16,64,360]{3,2,1,0:T(8,128)} %get-tuple-element.5.wind_ref), custom_call_target="tpu_custom_call" | custom-call | tf_op jit(solution)/shard_map/gradient/pallas_call | solution.py:575

commit v3 on v2

--- a/solution.py
+++ b/solution.py
@@ -130,11 +130,11 @@
 
 def far_kernel(
     cut_hbm, th_hbm, wind_hbm, near_hbm, short_hbm, early_hbm, late_hbm, cross_hbm,
-    ext_hbm, out_hbm,
-    cut_ref, th, w, ext, xs, turn, geo, wide, near, short, early, late, cross,
+    ext, w,
+    cut_ref, th, xs, turn, geo, wide, near, short, early, late, cross,
     inner, to_near, from_near, u, zin, vs, vr,
     lon_out, lon_in, lat_out, lat_in,
-    load_sem, near_sem, nearr_sem, u_sem, z_sem, v_sem, vr_sem, lon_sem, lonr_sem, lat_sem, latr_sem, done_sem,
+    load_sem, near_sem, nearr_sem, u_sem, z_sem, v_sem, vr_sem, lon_sem, lonr_sem, lat_sem, latr_sem,
 ):
     z, p = place()
     polar = (z < 2) | (z >= 6)
@@ -405,12 +405,9 @@
         remote, own = v_copy(p)
         own.start()
 
-        def step(i, carry):
+        for i in range(1, RING):
             remote, own = v_copy((p + i) % RING)
             remote.start()
-            return carry
-
-        lax.fori_loop(1, RING, step, 0)
 
     @pl.when(polar)
     def _():
@@ -458,9 +455,6 @@
                 return carry
 
             lax.fori_loop(0, PAIRS, step, 0)
-
-    out_copy = pltpu.make_async_copy(w, out_hbm, done_sem.at[0])
-    out_copy.start()
 
     wait_edges(1)
     for i in range(PAIRS):
@@ -470,8 +464,6 @@
     for lev in range(LEVELS):
         ext[lev, ROWS : ROWS + 1] = jnp.where(z == BANDS - 1, 0.0, lat_in[1, 1, lev : lev + 1])
         ext[lev, ROWS + 7 : ROWS + 8] = jnp.where(z == 0, 0.0, lat_in[1, 0, lev : lev + 1])
-    ext_copy = pltpu.make_async_copy(ext, ext_hbm, done_sem.at[1])
-    ext_copy.start()
 
     @pl.when(polar)
     def _():
@@ -497,24 +489,23 @@
         for k in range(4, 9):
             loads[k].wait()
 
-    out_copy.wait()
-    ext_copy.wait()
-
 
 def gradient_kernel(ext_ref, wind_ref, thick_ref, out_ref, geo):
     z, _ = place()
-
-    @pl.when(pl.program_id(0) == 0)
+    step = pl.program_id(0)
+
+    @pl.when(step == 0)
     def _():
         geo[...] = press_coef * latitude_tables(z, (ROWS, WIDE))[1]
 
     for k in range(STEP):
-        cells = ext_ref[k]
+        lev = step * STEP + k
+        cells = ext_ref[lev]
         lon_diff = pltpu.roll(cells, WIDE - 1, 1) - pltpu.roll(cells, 1, 1)
         lat_diff = pltpu.roll(cells, ROWS + 7, 0) - pltpu.roll(cells, 1, 0)
         thick_ref[k] = cells[0:ROWS, 0:COLS]
-        out_ref[0, k] = wind_ref[0, k] - (geo[...] * lon_diff[0:ROWS])[:, 0:COLS]
-        out_ref[1, k] = wind_ref[1, k] - (press_coef * lat_diff[0:ROWS])[:, 0:COLS]
+        out_ref[0, k] = wind_ref[0, lev] - (geo[...] * lon_diff[0:ROWS])[:, 0:COLS]
+        out_ref[1, k] = wind_ref[1, lev] - (press_coef * lat_diff[0:ROWS])[:, 0:COLS]
 
 
 def body(thickness, wind, cutoff, tables):
@@ -524,16 +515,14 @@
     ext, moved = pl.pallas_call(
         far_kernel,
         out_shape=(
-            jax.ShapeDtypeStruct((LEVELS, ROWS + 8, WIDE), F32),
-            jax.ShapeDtypeStruct((2, LEVELS, ROWS, COLS), F32),
+            pltpu.VMEM((LEVELS, ROWS + 8, WIDE), F32),
+            pltpu.VMEM((2, LEVELS, ROWS, COLS), F32),
         ),
-        in_specs=[any_space] * 8,
-        out_specs=(any_space, any_space),
+        in_specs=[pl.BlockSpec(memory_space=pltpu.HBM)] * 8,
+        out_specs=(pl.BlockSpec(memory_space=pltpu.VMEM),) * 2,
         scratch_shapes=[
             pltpu.VMEM((1, 4 * ROWS), jnp.int32),
             pltpu.VMEM((LEVELS, ROWS, COLS), F32),
-            pltpu.VMEM((2, LEVELS, ROWS, COLS), F32),
-            pltpu.VMEM((LEVELS, ROWS + 8, WIDE), F32),
             pltpu.VMEM((CHUNKS, 2 * ITEMS, 2 * WIDE), BF16),
             pltpu.VMEM((3, ITEMS, WIDE), F32),
             pltpu.VMEM((2, ITEMS, WIDE), F32),
@@ -565,10 +554,9 @@
             dma((2, 2)),
             dma((2, 2)),
             dma((2, 2)),
-            dma((2,)),
         ],
         compiler_params=pltpu.CompilerParams(
-            collective_id=0, has_side_effects=True, vmem_limit_bytes=60 * 2**20
+            collective_id=0, has_side_effects=True, vmem_limit_bytes=61865984
         ),
         name="far",
     )(cutoff.reshape(1, -1), thickness, wind, near, short, early, late, cross)
@@ -580,14 +568,15 @@
             jax.ShapeDtypeStruct((2, LEVELS, ROWS, COLS), F32),
         ),
         in_specs=[
-            pl.BlockSpec((STEP, ROWS + 8, WIDE), lambda i: (i, 0, 0)),
-            pl.BlockSpec((2, STEP, ROWS, COLS), lambda i: (0, i, 0, 0)),
+            pl.BlockSpec(memory_space=pltpu.VMEM),
+            pl.BlockSpec(memory_space=pltpu.VMEM),
         ],
         out_specs=(
             pl.BlockSpec((STEP, ROWS, COLS), lambda i: (i, 0, 0)),
             pl.BlockSpec((2, STEP, ROWS, COLS), lambda i: (0, i, 0, 0)),
         ),
         scratch_shapes=[pltpu.VMEM((ROWS, WIDE), F32)],
+        compiler_params=pltpu.CompilerParams(vmem_limit_bytes=40 * 2**20),
         name="gradient",
     )(ext, moved)
 

time: 47.4 us -> 43.4 us (0.916)
  Pallas kernels: 46.6 us -> 42.6 us
    pallas_call x1, Pallas kernels: 5.27 us -> 2.94 us  [body(): pl.pallas_call(gradient_kernel, grid=(LEVELS // STEP,), out_shape=(jax.Sh...]
    pallas_call x1, Pallas kernels: 41.3 us -> 39.7 us  [body(): pl.pallas_call(far_kernel, out_shape=(pltpu.VMEM((LEVELS, ROWS + 8, WIDE)...]
where the time goes in v3:
time: 43.4 us; the launch traced here: 43.3 us
  Pallas kernels  42.6 us (98%)
  between operations  0.64 us (1%)
    pallas_call x1, Pallas kernels, body(): pl.pallas_call(far_kernel, out_shape=(pltpu.VMEM((LEVELS, ROWS + 8, WIDE)...  39.7 us
    pallas_call x1, Pallas kernels, body(): pl.pallas_call(gradient_kernel, grid=(LEVELS // STEP,), out_shape=(jax.Sh...  2.94 us

profile of v3, /device:TPU:1, one launch (start us, length us, event | category | flops | bytes accessed | tf_op | source)
XLA Modules:
  0.0 43.3 jit_solution(15580519353794829735)
XLA Ops:
  0.6 39.7 %far.1 = (f32[16,72,384]{2,1,0:T(8,128)S(1)}, f32[2,16,64,360]{3,2,1,0:T(8,128)S(1)}) custom-call(s32[1,256]{1,0:T(1,128)} %bitcast.1, f32[16,64,360]{2,1,0:T(8,128)} %th_hbm.1, f32[2,16,64,360]{3,2,1,0:T(8,128)} %wind_hbm.1, bf16[256,256]{1,0:T(8,128)(2,1)} %constant.10.clone.near_hbm, bf16[176,768]{1,0:T(8,128)(2,1)} %constant.11.clone.short_hbm, ...), custom_call_target="tpu_custom_call" | custom-call | tf_op jit(solution)/shard_map/far/pallas_call | solution.py:515
  40.3 2.9 %gradient.1 = (f32[16,64,360]{2,1,0:T(8,128)}, f32[2,16,64,360]{3,2,1,0:T(8,128)}) custom-call(f32[16,72,384]{2,1,0:T(8,128)S(1)} %get-tuple-element.4.ext_ref, f32[2,16,64,360]{3,2,1,0:T(8,128)S(1)} %get-tuple-element.5.wind_ref), custom_call_target="tpu_custom_call" | custom-call | tf_op jit(solution)/shard_map/gradient/pallas_call | solution.py:563

commit v4 on v3

--- a/solution.py
+++ b/solution.py
@@ -32,6 +32,7 @@
 PAIRS = LEVELS // 2
 CHUNKS = 3 * PAIRS
 STEP = 4
+TOGETHER = 4
 ITEMS = 2 * ROWS
 
 
@@ -115,11 +116,12 @@
     return z, p
 
 
-def latitude_tables(z, shape):
-    row = lax.broadcasted_iota(jnp.int32, shape, 0) + z * ROWS
+def latitude_tables(z):
+    row = lax.broadcasted_iota(jnp.int32, (ROWS, 128), 0) + z * ROWS
     latitude = math.pi * ((row.astype(F32) + 0.5) / (ROWS * BANDS) - 0.5)
     cosine = jnp.cos(latitude)
-    return cosine, 1.0 / jnp.maximum(cosine, 0.2)
+    metric = 1.0 / jnp.maximum(cosine, 0.2)
+    return [jnp.concatenate([table] * (WIDE // 128), axis=1) for table in (cosine, metric)]
 
 
 def worker(phase, q):
@@ -149,19 +151,18 @@
         pltpu.make_async_copy(cross_hbm, cross, load_sem.at[7]),
         pltpu.make_async_copy(late_hbm, late, load_sem.at[8]),
     ]
-    for k in (3, 0, 1, 2, 4, 5, 6, 7, 8):
+    barrier = pltpu.get_barrier_semaphore()
+
+    for k in (3, 0, 1):
         loads[k].start()
-    barrier = pltpu.get_barrier_semaphore()
-
-    def greet(i, carry):
+    for i in range(1, RING):
         pl.semaphore_signal(barrier, inc=1, device_id=(z, (p + i) % RING), device_id_type=MESH)
-        return carry
-
-    lax.fori_loop(1, RING, greet, 0)
     for dz in (1, BANDS - 1):
         pl.semaphore_signal(barrier, inc=1, device_id=((z + dz) % BANDS, p), device_id_type=MESH)
-
-    cosine, metric = latitude_tables(z, (ROWS, WIDE))
+    for k in (2, 4, 5, 6, 7, 8):
+        loads[k].start()
+
+    cosine, metric = latitude_tables(z)
     for half in range(2):
         geo[0, half * ROWS : (half + 1) * ROWS] = cosine
         geo[1, half * ROWS : (half + 1) * ROWS] = advect_coef * metric
@@ -249,7 +250,20 @@
             )
         lat_copy(0, side, (1, BANDS - 1)[side]).start()
 
-    def shrink(ch, values):
+    def several(work):
+        def step(i, carry):
+            work([TOGETHER * i + k for k in range(TOGETHER)])
+            return carry
+
+        lax.fori_loop(0, PAIRS // TOGETHER, step, 0)
+
+    def shrink(chunks, values):
+        for ch, part in zip(chunks, values):
+            widen(ch, part)
+        for ch in chunks:
+            shorten(ch)
+
+    def widen(ch, values):
         for half in range(2):
             rows = slice(half * ITEMS, (half + 1) * ITEMS)
             high, low = split(values * turn[half, :, 0:COLS])
@@ -257,6 +271,8 @@
                 size = min(SUB, COLS - k * SUB)
                 xs[ch, rows, 2 * k * SUB : 2 * k * SUB + size] = high[:, k * SUB : k * SUB + size]
                 xs[ch, rows, (2 * k + 1) * SUB : (2 * k + 1) * SUB + size] = low[:, k * SUB : k * SUB + size]
+
+    def shorten(ch):
         both = dot(short[...], xs[ch], ((1,), (1,)))
         both = both[0:SHORT] + both[SHORT:]
         u[ch] = both[0:FAR]
@@ -299,33 +315,47 @@
         loads[4].wait()
         for phase in range(2):
 
-            def step(i, carry):
-                shrink(phase * PAIRS + i, w[phase, pl.ds(2 * i, 2)].reshape(ITEMS, COLS))
-                return carry
-
-            lax.fori_loop(0, PAIRS, step, 0)
+            several(
+                lambda parts: shrink(
+                    [phase * PAIRS + i for i in parts],
+                    [w[phase, pl.ds(2 * i, 2)].reshape(ITEMS, COLS) for i in parts],
+                )
+            )
             send_u(phase)
             for side in range(2):
                 near_copy(phase, side).start()
 
-    wait_edges(0)
     row_index = lax.broadcasted_iota(jnp.int32, (ROWS, WIDE), 0)
     for i in range(PAIRS):
         pair = slice(2 * i, 2 * i + 2)
         wide[:, 0:COLS] = (th[pair] * w[0, pair]).reshape(ITEMS, COLS)
-        flux = jnp.concatenate([wide[:, 0:256], with_edges(0, i, wide[:, 256:WIDE])], axis=1)
+        flux = wide[...]
         lon_diff = pltpu.roll(flux, WIDE - 1, 1) - pltpu.roll(flux, 1, 1)
         wide[:, 0:COLS] = (th[pair] * w[1, pair]).reshape(ITEMS, COLS)
         flux = wide[...] * geo[0]
         for k in range(2):
             lev = 2 * i + k
             cells = flux[k * ROWS : (k + 1) * ROWS]
-            south = jnp.where(z == 0, 0.0, lat_in[0, 0, lev : lev + 1])
-            north = jnp.where(z == BANDS - 1, 0.0, lat_in[0, 1, lev : lev + 1])
-            up = jnp.where(row_index == ROWS - 1, north, pltpu.roll(cells, ROWS - 1, 0))
-            down = jnp.where(row_index == 0, south, pltpu.roll(cells, 1, 0))
+            up = jnp.where(row_index == ROWS - 1, 0.0, pltpu.roll(cells, ROWS - 1, 0))
+            down = jnp.where(row_index == 0, 0.0, pltpu.roll(cells, 1, 0))
             change = geo[1, 0:ROWS] * (lon_diff[k * ROWS : (k + 1) * ROWS] + (up - down))
             th[lev] = th[lev] - change[:, 0:COLS]
+    wait_edges(0)
+    last_lane = lax.broadcasted_iota(jnp.int32, (ITEMS, COLS - 256), 1)
+    for i in range(PAIRS):
+        pair = slice(2 * i, 2 * i + 2)
+        left = lon_in[0, 0, :, PAIRS + i : PAIRS + i + 1] * geo[1, :, 0:128]
+        right = lon_in[0, 1, :, i : i + 1] * geo[1, :, 0 : COLS - 256]
+        tile = th[pair, :, 0:128].reshape(ITEMS, 128)
+        th[pair, :, 0:128] = jnp.where(lane == 0, tile + left, tile).reshape(2, ROWS, 128)
+        tile = th[pair, :, 256:COLS].reshape(ITEMS, COLS - 256)
+        tile = jnp.where(last_lane == COLS - 257, tile - right, tile)
+        th[pair, :, 256:COLS] = tile.reshape(2, ROWS, COLS - 256)
+    for lev in range(LEVELS):
+        south = jnp.where(z == 0, 0.0, lat_in[0, 0, lev : lev + 1, 0:COLS])
+        north = jnp.where(z == BANDS - 1, 0.0, lat_in[0, 1, lev : lev + 1, 0:COLS])
+        th[lev, 0:1] = th[lev, 0:1] + geo[1, 0:1, 0:COLS] * south
+        th[lev, ROWS - 1 : ROWS] = th[lev, ROWS - 1 : ROWS] - geo[1, ROWS - 1 : ROWS, 0:COLS] * north
 
     first_sign = jnp.where(p == 0, -1.0, 1.0).astype(F32)
     last_sign = jnp.where(p == RING - 1, -1.0, 1.0).astype(F32)
@@ -349,16 +379,21 @@
         for side in range(2):
             near_copy(phase, side).wait()
 
-        def step(i, carry):
-            pair = pl.ds(2 * i, 2)
-            result = local(phase * PAIRS + i, w[phase, pair].reshape(ITEMS, COLS))
-            w[phase, pair] = result.reshape(2, ROWS, COLS)
-            return carry
-
-        lax.fori_loop(0, PAIRS, step, 0)
+        def work(parts):
+            pairs = [pl.ds(2 * i, 2) for i in parts]
+            results = [
+                local(phase * PAIRS + i, w[phase, pair].reshape(ITEMS, COLS)) for i, pair in zip(parts, pairs)
+            ]
+            for pair, result in zip(pairs, results):
+                w[phase, pair] = result.reshape(2, ROWS, COLS)
+
+        several(work)
+
+    def arrived(chunks):
+        for ch in chunks:
+            pltpu.make_async_copy(vr.at[ch], vr.at[ch], vr_sem.at[ch]).wait()
 
     def grown(ch):
-        pltpu.make_async_copy(vr.at[ch], vr.at[ch], vr_sem.at[ch]).wait()
         values = vr[ch]
         high = values.astype(BF16).astype(F32)
         stack = jnp.concatenate([high, values - high, high, jnp.zeros((FAR, 2 * ITEMS), F32)], axis=0).astype(BF16)
@@ -380,11 +415,12 @@
 
     @pl.when(polar)
     def _():
-        def step(i, carry):
-            shrink(2 * PAIRS + i, th[pl.ds(2 * i, 2)].reshape(ITEMS, COLS))
-            return carry
-
-        lax.fori_loop(0, PAIRS, step, 0)
+        several(
+            lambda parts: shrink(
+                [2 * PAIRS + i for i in parts],
+                [th[pl.ds(2 * i, 2)].reshape(ITEMS, COLS) for i in parts],
+            )
+        )
         send_u(2)
         for side in range(2):
             near_copy(2, side).start()
@@ -411,23 +447,25 @@
 
     @pl.when(polar)
     def _():
-        local_wind(1)
         for side in range(2):
             near_copy(2, side).wait()
 
-        def local_thick(i, carry):
-            pair = pl.ds(2 * i, 2)
-            th[pair] = local(2 * PAIRS + i, th[pair].reshape(ITEMS, COLS)).reshape(2, ROWS, COLS)
-            return carry
-
-        lax.fori_loop(0, PAIRS, local_thick, 0)
-
-        def step(i, carry):
-            pair = pl.ds(2 * i, 2)
-            ext[pair, 0:ROWS, 0:COLS] = th[pair] + grown(2 * PAIRS + i)
-            return carry
-
-        lax.fori_loop(0, PAIRS, step, 0)
+        def local_thick(parts):
+            pairs = [pl.ds(2 * i, 2) for i in parts]
+            results = [local(2 * PAIRS + i, th[pair].reshape(ITEMS, COLS)) for i, pair in zip(parts, pairs)]
+            for pair, result in zip(pairs, results):
+                th[pair] = result.reshape(2, ROWS, COLS)
+
+        several(local_thick)
+
+        def work(parts):
+            arrived([2 * PAIRS + i for i in parts])
+            pairs = [pl.ds(2 * i, 2) for i in parts]
+            results = [th[pair] + grown(2 * PAIRS + i) for i, pair in zip(parts, pairs)]
+            for pair, result in zip(pairs, results):
+                ext[pair, 0:ROWS, 0:COLS] = result
+
+        several(work)
 
     @pl.when(jnp.logical_not(polar))
     def _():
@@ -447,14 +485,17 @@
 
     @pl.when(polar)
     def _():
+        local_wind(1)
         for phase in range(2):
 
-            def step(i, carry):
-                pair = pl.ds(2 * i, 2)
-                w[phase, pair] = w[phase, pair] + grown(phase * PAIRS + i)
-                return carry
-
-            lax.fori_loop(0, PAIRS, step, 0)
+            def work(parts):
+                arrived([phase * PAIRS + i for i in parts])
+                pairs = [pl.ds(2 * i, 2) for i in parts]
+                results = [w[phase, pair] + grown(phase * PAIRS + i) for i, pair in zip(parts, pairs)]
+                for pair, result in zip(pairs, results):
+                    w[phase, pair] = result
+
+            several(work)
 
     wait_edges(1)
     for i in range(PAIRS):
@@ -496,7 +537,7 @@
 
     @pl.when(step == 0)
     def _():
-        geo[...] = press_coef * latitude_tables(z, (ROWS, WIDE))[1]
+        geo[...] = press_coef * latitude_tables(z)[1]
 
     for k in range(STEP):
         lev = step * STEP + k

time: 43.4 us -> 36.4 us (0.84)
  Pallas kernels: 42.6 us -> 35.6 us
    pallas_call x1, Pallas kernels: 39.7 us -> 32.7 us  [body(): pl.pallas_call(far_kernel, out_shape=(pltpu.VMEM((LEVELS, ROWS + 8, WIDE)...]
where the time goes in v4:
time: 36.4 us; the launch traced here: 36.3 us
  Pallas kernels  35.6 us (98%)
  between operations  0.64 us (2%)
    pallas_call x1, Pallas kernels, body(): pl.pallas_call(far_kernel, out_shape=(pltpu.VMEM((LEVELS, ROWS + 8, WIDE)...  32.7 us
    pallas_call x1, Pallas kernels, body(): pl.pallas_call(gradient_kernel, grid=(LEVELS // STEP,), out_shape=(jax.Sh...  2.94 us

profile of v4, /device:TPU:1, one launch (start us, length us, event | category | flops | bytes accessed | tf_op | source)
XLA Modules:
  0.0 36.3 jit_solution(1498989703245258473)
XLA Ops:
  0.6 32.7 %far.1 = (f32[16,72,384]{2,1,0:T(8,128)S(1)}, f32[2,16,64,360]{3,2,1,0:T(8,128)S(1)}) custom-call(s32[1,256]{1,0:T(1,128)} %bitcast.1, f32[16,64,360]{2,1,0:T(8,128)} %th_hbm.1, f32[2,16,64,360]{3,2,1,0:T(8,128)} %wind_hbm.1, bf16[256,256]{1,0:T(8,128)(2,1)} %constant.10.clone.near_hbm, bf16[176,768]{1,0:T(8,128)(2,1)} %constant.11.clone.short_hbm, ...), custom_call_target="tpu_custom_call" | custom-call | tf_op jit(solution)/shard_map/far/pallas_call | solution.py:556
  33.3 2.9 %gradient.1 = (f32[16,64,360]{2,1,0:T(8,128)}, f32[2,16,64,360]{3,2,1,0:T(8,128)}) custom-call(f32[16,72,384]{2,1,0:T(8,128)S(1)} %get-tuple-element.4.ext_ref, f32[2,16,64,360]{3,2,1,0:T(8,128)S(1)} %get-tuple-element.5.wind_ref), custom_call_target="tpu_custom_call" | custom-call | tf_op jit(solution)/shard_map/gradient/pallas_call | solution.py:604

commit v5 on v4

--- a/solution.py
+++ b/solution.py
@@ -166,7 +166,7 @@
     for half in range(2):
         geo[0, half * ROWS : (half + 1) * ROWS] = cosine
         geo[1, half * ROWS : (half + 1) * ROWS] = advect_coef * metric
-    wide[...] = jnp.zeros((ITEMS, WIDE), F32)
+    wide[...] = jnp.zeros((4, ITEMS, WIDE), F32)
 
     loads[3].wait()
 
@@ -328,11 +328,12 @@
     row_index = lax.broadcasted_iota(jnp.int32, (ROWS, WIDE), 0)
     for i in range(PAIRS):
         pair = slice(2 * i, 2 * i + 2)
-        wide[:, 0:COLS] = (th[pair] * w[0, pair]).reshape(ITEMS, COLS)
-        flux = wide[...]
+        first, second = 2 * (i % 2), 2 * (i % 2) + 1
+        wide[first, :, 0:COLS] = (th[pair] * w[0, pair]).reshape(ITEMS, COLS)
+        wide[second, :, 0:COLS] = (th[pair] * w[1, pair]).reshape(ITEMS, COLS)
+        flux = wide[first]
         lon_diff = pltpu.roll(flux, WIDE - 1, 1) - pltpu.roll(flux, 1, 1)
-        wide[:, 0:COLS] = (th[pair] * w[1, pair]).reshape(ITEMS, COLS)
-        flux = wide[...] * geo[0]
+        flux = wide[second] * geo[0]
         for k in range(2):
             lev = 2 * i + k
             cells = flux[k * ROWS : (k + 1) * ROWS]
@@ -531,22 +532,29 @@
             loads[k].wait()
 
 
-def gradient_kernel(ext_ref, wind_ref, thick_ref, out_ref, geo):
+def gradient_kernel(ext_ref, wind_ref, thick_hbm, out_hbm, thick, out, done_sem):
     z, _ = place()
-    step = pl.program_id(0)
-
-    @pl.when(step == 0)
-    def _():
-        geo[...] = press_coef * latitude_tables(z)[1]
-
-    for k in range(STEP):
-        lev = step * STEP + k
-        cells = ext_ref[lev]
-        lon_diff = pltpu.roll(cells, WIDE - 1, 1) - pltpu.roll(cells, 1, 1)
-        lat_diff = pltpu.roll(cells, ROWS + 7, 0) - pltpu.roll(cells, 1, 0)
-        thick_ref[k] = cells[0:ROWS, 0:COLS]
-        out_ref[0, k] = wind_ref[0, lev] - (geo[...] * lon_diff[0:ROWS])[:, 0:COLS]
-        out_ref[1, k] = wind_ref[1, lev] - (press_coef * lat_diff[0:ROWS])[:, 0:COLS]
+    slope = press_coef * latitude_tables(z)[1]
+    copies = []
+    for first in range(0, LEVELS, STEP):
+        for lev in range(first, first + STEP):
+            cells = ext_ref[lev]
+            lon_diff = pltpu.roll(cells, WIDE - 1, 1) - pltpu.roll(cells, 1, 1)
+            lat_diff = pltpu.roll(cells, ROWS + 7, 0) - pltpu.roll(cells, 1, 0)
+            thick[lev] = cells[0:ROWS, 0:COLS]
+            out[0, lev] = wind_ref[0, lev] - (slope * lon_diff[0:ROWS])[:, 0:COLS]
+            out[1, lev] = wind_ref[1, lev] - (press_coef * lat_diff[0:ROWS])[:, 0:COLS]
+        part = pl.ds(first, STEP)
+        group = first // STEP
+        copies += [
+            pltpu.make_async_copy(thick.at[part], thick_hbm.at[part], done_sem.at[0, group]),
+            pltpu.make_async_copy(out.at[0, part], out_hbm.at[0, part], done_sem.at[1, group]),
+            pltpu.make_async_copy(out.at[1, part], out_hbm.at[1, part], done_sem.at[2, group]),
+        ]
+        for copy in copies[-3:]:
+            copy.start()
+    for copy in copies:
+        copy.wait()
 
 
 def body(thickness, wind, cutoff, tables):
@@ -567,7 +575,7 @@
             pltpu.VMEM((CHUNKS, 2 * ITEMS, 2 * WIDE), BF16),
             pltpu.VMEM((3, ITEMS, WIDE), F32),
             pltpu.VMEM((2, ITEMS, WIDE), F32),
-            pltpu.VMEM((ITEMS, WIDE), F32),
+            pltpu.VMEM((4, ITEMS, WIDE), F32),
             pltpu.VMEM(near.shape, BF16),
             pltpu.VMEM(short.shape, BF16),
             pltpu.VMEM(early.shape, BF16),
@@ -603,20 +611,17 @@
     )(cutoff.reshape(1, -1), thickness, wind, near, short, early, late, cross)
     return pl.pallas_call(
         gradient_kernel,
-        grid=(LEVELS // STEP,),
         out_shape=(
             jax.ShapeDtypeStruct((LEVELS, ROWS, COLS), F32),
             jax.ShapeDtypeStruct((2, LEVELS, ROWS, COLS), F32),
         ),
-        in_specs=[
-            pl.BlockSpec(memory_space=pltpu.VMEM),
-            pl.BlockSpec(memory_space=pltpu.VMEM),
+        in_specs=[pl.BlockSpec(memory_space=pltpu.VMEM)] * 2,
+        out_specs=(any_space, any_space),
+        scratch_shapes=[
+            pltpu.VMEM((LEVELS, ROWS, COLS), F32),
+            pltpu.VMEM((2, LEVELS, ROWS, COLS), F32),
+            dma((3, LEVELS // STEP)),
         ],
-        out_specs=(
-            pl.BlockSpec((STEP, ROWS, COLS), lambda i: (i, 0, 0)),
-            pl.BlockSpec((2, STEP, ROWS, COLS), lambda i: (0, i, 0, 0)),
-        ),
-        scratch_shapes=[pltpu.VMEM((ROWS, WIDE), F32)],
         compiler_params=pltpu.CompilerParams(vmem_limit_bytes=40 * 2**20),
         name="gradient",
     )(ext, moved)

time: 36.4 us -> 35.9 us (0.986)
  Pallas kernels: 35.6 us -> 35.1 us
    pallas_call x1, Pallas kernels: 2.94 us -> 2.5 us  [body(): pl.pallas_call(gradient_kernel, out_shape=(jax.ShapeDtypeStruct((LEVELS,...]
where the time goes in v5:
time: 35.9 us; the launch traced here: 35.8 us
  Pallas kernels  35.1 us (98%)
  between operations  0.64 us (2%)
    pallas_call x1, Pallas kernels, body(): pl.pallas_call(far_kernel, out_shape=(pltpu.VMEM((LEVELS, ROWS + 8, WIDE)...  32.6 us
    pallas_call x1, Pallas kernels, body(): pl.pallas_call(gradient_kernel, out_shape=(jax.ShapeDtypeStruct((LEVELS,...  2.5 us

profile of v5, /device:TPU:1, one launch (start us, length us, event | category | flops | bytes accessed | tf_op | source)
XLA Modules:
  0.0 35.8 jit_solution(5927928089371754154)
XLA Ops:
  0.6 32.6 %far.1 = (f32[16,72,384]{2,1,0:T(8,128)S(1)}, f32[2,16,64,360]{3,2,1,0:T(8,128)S(1)}) custom-call(s32[1,256]{1,0:T(1,128)} %bitcast.1, f32[16,64,360]{2,1,0:T(8,128)} %th_hbm.1, f32[2,16,64,360]{3,2,1,0:T(8,128)} %wind_hbm.1, bf16[256,256]{1,0:T(8,128)(2,1)} %constant.10.clone.near_hbm, bf16[176,768]{1,0:T(8,128)(2,1)} %constant.11.clone.short_hbm, ...), custom_call_target="tpu_custom_call" | custom-call | tf_op jit(solution)/shard_map/far/pallas_call | solution.py:564
  33.3 2.5 %gradient.1 = (f32[16,64,360]{2,1,0:T(8,128)}, f32[2,16,64,360]{3,2,1,0:T(8,128)}) custom-call(f32[16,72,384]{2,1,0:T(8,128)S(1)} %get-tuple-element.4.ext_ref, f32[2,16,64,360]{3,2,1,0:T(8,128)S(1)} %get-tuple-element.5.wind_ref), custom_call_target="tpu_custom_call" | custom-call | tf_op jit(solution)/shard_map/gradient/pallas_call | solution.py:612
